TPU v7x, 32 devices: a whole 2x2x4 slice. The times are simulated.
32 devices in a mesh: shard: 8 (over z, x), ctx: 2 (over y), tp: 2 (over core).
Axes of the slice: x: 2, y: 2, z: 4, core: 2. Of those that a mesh axis runs over, the one named last changes fastest.
Arguments:
- tokens: bfloat16 [16, 1024, 1024], P('shard', 'ctx'), may hold values from -6 to 6
- segments: int32 [16, 1024], P('shard'), may hold values from 0 to 3, as said below
- cotangent: bfloat16 [16, 1024, 1024], P('shard', 'ctx'), may hold values from -6 to 6
- mix_gain: float32 [1024], replicated, may hold values from 0.5 to 1.5
- ffn_gain: float32 [1024], replicated, may hold values from 0.5 to 1.5
- ssm_gate: bfloat16 [1024, 1536], P(('shard', 'ctx'), 'tp'), may hold values from -0.1875 to 0.1875
- ssm_input: bfloat16 [1024, 1536], P(('shard', 'ctx'), 'tp'), may hold values from -0.1875 to 0.1875
- ssm_state: bfloat16 [1024, 256], P(('shard', 'ctx')), may hold values from -0.1875 to 0.1875
- ssm_step: bfloat16 [1024, 24], P(('shard', 'ctx'), 'tp'), may hold values from -0.1875 to 0.1875
- attn_query: bfloat16 [1024, 512], P(('shard', 'ctx'), 'tp'), may hold values from -0.1875 to 0.1875
- attn_keyval: bfloat16 [1024, 2, 128], P(('shard', 'ctx'), 'tp'), may hold values from -0.1875 to 0.1875
- ssm_out: bfloat16 [1536, 1024], P('tp', ('shard', 'ctx')), may hold values from -0.109375 to 0.109375
- attn_out: bfloat16 [512, 1024], P('tp', ('shard', 'ctx')), may hold values from -3 to 3
- ffn_gate: bfloat16 [1024, 2048], P(('shard', 'ctx'), 'tp'), may hold values from -0.1875 to 0.1875
- ffn_up: bfloat16 [1024, 2048], P(('shard', 'ctx'), 'tp'), may hold values from -0.1875 to 0.1875
- ffn_down: bfloat16 [2048, 1024], P('tp', ('shard', 'ctx')), may hold values from -0.125 to 0.125
- conv_input: float32 [4, 1536], P(None, 'tp'), may hold values from -2.5 to 2.5
- conv_state: float32 [4, 256], replicated, may hold values from -2.5 to 2.5
- step_bias: float32 [24], P('tp'), may hold values from -1.5 to 0.5
- decay_rate: float32 [24], P('tp'), may hold values from 0.0009765625 to 0.05
Outputs:
- layer_out: bfloat16 [16, 1024, 1024], P('shard', 'ctx')
- grad_tokens: float32 [16, 1024, 1024], P('shard', 'ctx')
- grad_mix_gain: float32 [1024], replicated
- grad_ffn_gain: float32 [1024], replicated
- grad_ssm_gate: float32 [1024, 1536], P(('shard', 'ctx'), 'tp')
- grad_ssm_input: float32 [1024, 1536], P(('shard', 'ctx'), 'tp')
- grad_ssm_state: float32 [1024, 256], P(('shard', 'ctx'))
- grad_ssm_step: float32 [1024, 24], P(('shard', 'ctx'), 'tp')
- grad_attn_query: float32 [1024, 512], P(('shard', 'ctx'), 'tp')
- grad_attn_keyval: float32 [1024, 2, 128], P(('shard', 'ctx'), 'tp')
- grad_ssm_out: float32 [1536, 1024], P('tp', ('shard', 'ctx'))
- grad_attn_out: float32 [512, 1024], P('tp', ('shard', 'ctx'))
- grad_ffn_gate: float32 [1024, 2048], P(('shard', 'ctx'), 'tp')
- grad_ffn_up: float32 [1024, 2048], P(('shard', 'ctx'), 'tp')
- grad_ffn_down: float32 [2048, 1024], P('tp', ('shard', 'ctx'))
- grad_conv_input: float32 [4, 1536], P(None, 'tp')
- grad_conv_state: float32 [4, 256], replicated
- grad_step_bias: float32 [24], P('tp')
- grad_decay_rate: float32 [24], P('tp')
Inputs may be any that keep to these rules, and one draw needn't show every extreme that they name: `segments`: along each sequence the ids start at 0 and never fall; of the 2 sequences at each index of shard, one keeps id 0 up to position 768 or later.
All inputs are finite; a program needn't handle non-finite values.
Results may differ from a plain program's by a relative error of at most 0.019.
Values may be sent and summed in bfloat16 or wider, within the bound.
A program may use at most 192 MiB of HBM per device.

v0:
```python
import jax
import jax.numpy as jnp
from jax import lax
from jax.sharding import PartitionSpec as P

epsilon = 1e-05
highest = lax.Precision.HIGHEST


def shifted(block, axis, distance):
    devices = range(lax.axis_size(axis))
    route = [(i - distance, i) for i in devices if i - distance in devices]
    return lax.ppermute(block, axis, route)


def entering(value, axis, combine, identity, reverse):
    count, index = (lax.axis_size(axis), lax.axis_index(axis))
    everything = jax.tree.map(
        lambda part, kind: lax.all_gather(part.astype(kind), axis),
        value,
        (jnp.bfloat16, jnp.bfloat16),
    )
    start = jax.tree.map(
        lambda part, zero: jnp.broadcast_to(jnp.asarray(zero, part.dtype), part.shape),
        value,
        identity,
    )

    def step(k, before):
        at = count - 1 - k if reverse else k
        reached = at > index if reverse else at < index
        new = combine(
            before, jax.tree.map(lambda part, own: part[at].astype(own.dtype), everything, value)
        )
        return jax.tree.map(lambda a, b: jnp.where(reached, a, b), new, before)

    return lax.fori_loop(0, count, step, start)


def matmul(left_side, right_side):
    return jnp.dot(left_side, right_side, preferred_element_type=jnp.float32)


def weight_grad(left_side, right_side):
    return lax.dot_general(
        left_side, right_side, (((0,), (0,)), ((), ())), preferred_element_type=jnp.float32
    )


def back_product(left_side, right_side):
    return lax.dot_general(
        left_side, right_side, (((1,), (1,)), ((), ())), preferred_element_type=jnp.float32
    )


def rotary_tables(positions, head_dim):
    half_dim = head_dim // 2
    frequency = 10000.0 ** (-2.0 * jnp.arange(half_dim, dtype=jnp.float32) / head_dim)
    angles = positions.astype(jnp.float32)[:, None] * frequency[None, :]
    return (jnp.cos(angles), jnp.sin(angles))


def rotate(values, cos_table, sin_table):
    half_dim = values.shape[-1] // 2
    first_half = values[..., :half_dim]
    second_half = values[..., half_dim:]
    return jnp.concatenate(
        [
            first_half * cos_table - second_half * sin_table,
            second_half * cos_table + first_half * sin_table,
        ],
        axis=-1,
    )


def rotate_back(grads_in, cos_table, sin_table):
    half_dim = grads_in.shape[-1] // 2
    first_half = grads_in[..., :half_dim]
    second_half = grads_in[..., half_dim:]
    return jnp.concatenate(
        [
            first_half * cos_table + second_half * sin_table,
            second_half * cos_table - first_half * sin_table,
        ],
        axis=-1,
    )


def span_states(inner_act, input_mat, step_size, decay_rate, seg_part, seg_before):
    cumulative = jnp.cumsum(-step_size * decay_rate, axis=1)
    at_end = (seg_part == seg_part[:, -1:])[..., None]
    tail_decay = jnp.where(at_end, jnp.exp(cumulative[:, -1:, :] - cumulative), 0.0)
    weighted = inner_act * (tail_decay * step_size)[..., None]
    states = jnp.einsum("stha,stn->shan", weighted, input_mat, precision=highest)
    linked = (seg_part[:, -1] == seg_before)[:, None]
    linkage = jnp.where(linked, jnp.exp(cumulative[:, -1, :]), 0.0)
    return (states, linkage, cumulative)


def span_outputs(
    inner_act, input_mat, output_mat, step_size, seg_part, seg_before, cumulative, incoming
):
    length = inner_act.shape[1]
    ordinal = jnp.arange(length)
    allowed = (seg_part[:, :, None] == seg_part[:, None, :]) & (
        ordinal[:, None] >= ordinal[None, :]
    )[None]
    allowed = allowed[..., None]
    spread = cumulative[:, :, None, :] - cumulative[:, None, :, :]
    decays = jnp.where(allowed, jnp.exp(jnp.where(allowed, spread, 0.0)), 0.0)
    intersection = jnp.einsum("stn,sun->stu", output_mat, input_mat, precision=highest)
    mixing = intersection[..., None] * decays * step_size[:, None, :, :]
    local_part = jnp.einsum("stuh,suha->stha", mixing, inner_act, precision=highest)
    entrance = jnp.where((seg_part == seg_before[:, None])[..., None], jnp.exp(cumulative), 0.0)
    carried = (
        jnp.einsum("shan,stn->stha", incoming, output_mat, precision=highest) * entrance[..., None]
    )
    return local_part + carried


def combine_state(earlier, later):
    return (earlier[0] * later[0], later[0][..., None, None] * earlier[1] + later[1])


def conv_back(grad_conv, padded, conv_taps):
    tap_count = conv_taps.shape[0]
    length = grad_conv.shape[1]
    tap_grads = []
    grad_padded = jnp.zeros(padded.shape, jnp.float32)
    for tap_index in range(tap_count):
        tap_grads.append(
            jnp.sum(grad_conv * padded[:, tap_index : tap_index + length], axis=(0, 1))
        )
        grad_padded = grad_padded + jnp.pad(
            grad_conv * conv_taps[tap_index],
            ((0, 0), (tap_index, tap_count - 1 - tap_index), (0, 0)),
        )
    return (jnp.stack(tap_grads), grad_padded)


def add_rim(grad_padded, from_next, tap_count):
    own_part = grad_padded[:, tap_count - 1 :]
    length = own_part.shape[1]
    return jnp.concatenate(
        [own_part[:, : length - tap_count + 1], own_part[:, length - tap_count + 1 :] + from_next],
        axis=1,
    )


def attend_mask(seg_row, seg_part, offset):
    query_pos = offset + jnp.arange(seg_part.shape[0])
    key_pos = jnp.arange(seg_row.shape[0])
    return (query_pos[:, None] >= key_pos[None, :]) & (seg_part[:, None] == seg_row[None, :])


def attend_scores(queries, keyval, seg_row, seg_part, offset):
    head_dim = keyval.shape[1] // 2
    scores = jnp.einsum(
        "tqd,ud->qtu", queries, keyval[:, :head_dim], preferred_element_type=jnp.float32
    ) * head_dim ** (-0.5)
    allowed = attend_mask(seg_row, seg_part, offset)
    return jnp.where(allowed[None], scores, -1e30)


def attend_forward(queries, keyval, seg_row, seg_part, offset):
    head_dim = keyval.shape[1] // 2
    scores = attend_scores(queries, keyval, seg_row, seg_part, offset)
    largest = jnp.max(scores, axis=-1, keepdims=True)
    log_total = largest + jnp.log(jnp.sum(jnp.exp(scores - largest), axis=-1, keepdims=True))
    attn_probs = jnp.exp(scores - log_total).astype(jnp.bfloat16)
    attended = jnp.einsum(
        "qtu,ud->tqd", attn_probs, keyval[:, head_dim:], preferred_element_type=jnp.float32
    )
    return (attended, log_total)


def attend_backward(queries, keyval, seg_row, seg_part, log_total, grad_out, offset):
    head_dim = keyval.shape[1] // 2
    scale_factor = head_dim ** (-0.5)
    scores = attend_scores(queries, keyval, seg_row, seg_part, offset)
    attn_probs = jnp.exp(scores - log_total)
    probs_low = attn_probs.astype(jnp.bfloat16)
    grad_probs = jnp.einsum(
        "tqd,ud->qtu", grad_out, keyval[:, head_dim:], preferred_element_type=jnp.float32
    )
    inner_sum = jnp.sum(grad_probs * attn_probs, axis=-1, keepdims=True)
    grad_scores = (attn_probs * (grad_probs - inner_sum)).astype(jnp.bfloat16)
    grad_query = (
        jnp.einsum(
            "qtu,ud->tqd", grad_scores, keyval[:, :head_dim], preferred_element_type=jnp.float32
        )
        * scale_factor
    )
    grad_keys = (
        jnp.einsum("qtu,tqd->ud", grad_scores, queries, preferred_element_type=jnp.float32)
        * scale_factor
    )
    grad_vals = jnp.einsum("qtu,tqd->ud", probs_low, grad_out, preferred_element_type=jnp.float32)
    return (grad_query, jnp.concatenate([grad_keys, grad_vals], axis=1))


def fetch_weights(
    ssm_gate,
    ssm_input,
    ssm_state,
    ssm_step,
    attn_query,
    attn_keyval,
    ssm_out,
    attn_out,
    ffn_gate,
    ffn_up,
    ffn_down,
):
    return (
        lax.all_gather(ssm_gate, ("shard", "ctx"), axis=0, tiled=True),
        lax.all_gather(ssm_input, ("shard", "ctx"), axis=0, tiled=True),
        lax.all_gather(ssm_state, ("shard", "ctx"), axis=0, tiled=True),
        lax.all_gather(ssm_step, ("shard", "ctx"), axis=0, tiled=True),
        lax.all_gather(attn_query, ("shard", "ctx"), axis=0, tiled=True),
        lax.all_gather(attn_keyval, ("shard", "ctx"), axis=0, tiled=True),
        lax.all_gather(ssm_out, ("shard", "ctx"), axis=1, tiled=True),
        lax.all_gather(attn_out, ("shard", "ctx"), axis=1, tiled=True),
        lax.all_gather(ffn_gate, ("shard", "ctx"), axis=0, tiled=True),
        lax.all_gather(ffn_up, ("shard", "ctx"), axis=0, tiled=True),
        lax.all_gather(ffn_down, ("shard", "ctx"), axis=1, tiled=True),
    )


def fetch_keys(keyval_low):
    return lax.all_gather(keyval_low, "ctx", axis=1, tiled=True)


def shards(
    tokens,
    segments,
    cotangent,
    mix_gain,
    ffn_gain,
    ssm_gate,
    ssm_input,
    ssm_state,
    ssm_step,
    attn_query,
    attn_keyval,
    ssm_out,
    attn_out,
    ffn_gate,
    ffn_up,
    ffn_down,
    conv_input,
    conv_state,
    step_bias,
    decay_rate,
):
    seq_count, span_len, model_width = tokens.shape
    row_count = seq_count * span_len
    local_heads = step_bias.shape[0]
    inner_width = conv_input.shape[1]
    head_size = inner_width // local_heads
    state_width = conv_state.shape[1] // 2
    tap_count = conv_input.shape[0]
    head_dim = attn_keyval.shape[2] // 2
    query_width = attn_query.shape[1]
    query_heads = query_width // head_dim
    offset = lax.axis_index("ctx") * span_len
    gathered = fetch_weights(
        ssm_gate,
        ssm_input,
        ssm_state,
        ssm_step,
        attn_query,
        attn_keyval,
        ssm_out,
        attn_out,
        ffn_gate,
        ffn_up,
        ffn_down,
    )
    (
        full_gate,
        full_input,
        full_state,
        full_step,
        full_query,
        full_keyval,
        full_mixout,
        full_attnout,
        full_ffngate,
        full_ffnup,
        full_ffndown,
    ) = gathered
    keyval_flat = full_keyval.reshape(model_width, 2 * head_dim)
    inputs = tokens.reshape(row_count, model_width).astype(jnp.float32)
    inv_rms = lax.rsqrt(jnp.mean(inputs * inputs, axis=1, keepdims=True) + epsilon)
    normed = (inputs * inv_rms * mix_gain).astype(jnp.bfloat16)
    gate_lin = matmul(normed, full_gate)
    mixer_low = jnp.concatenate(
        [matmul(normed, full_input), matmul(normed, full_state)], axis=1
    ).astype(jnp.bfloat16)
    mixer_low = mixer_low.reshape(seq_count, span_len, inner_width + 2 * state_width)
    step_lin = matmul(normed, full_step)
    queries = matmul(normed, full_query)
    keyval = matmul(normed, keyval_flat)
    rim_rows = shifted(mixer_low[:, span_len - tap_count + 1 :], "ctx", 1)
    padded = jnp.concatenate([rim_rows, mixer_low], axis=1).astype(jnp.float32)
    conv_taps = jnp.concatenate([conv_input, conv_state], axis=1)
    conv_sum = padded[:, 0:span_len] * conv_taps[0]
    for tap_index in range(1, tap_count):
        conv_sum = conv_sum + padded[:, tap_index : tap_index + span_len] * conv_taps[tap_index]
    activated = jax.nn.silu(conv_sum)
    inner_act = activated[..., :inner_width].reshape(seq_count, span_len, local_heads, head_size)
    input_mat = activated[..., inner_width : inner_width + state_width]
    output_mat = activated[..., inner_width + state_width :]
    step_size = jax.nn.softplus(step_lin + step_bias).reshape(seq_count, span_len, local_heads)
    seg_part = lax.dynamic_slice_in_dim(segments, offset, span_len, 1)
    seg_prior = lax.dynamic_slice_in_dim(segments, jnp.maximum(offset - 1, 0), 1, 1)[:, 0]
    seg_before = jnp.where(offset > 0, seg_prior, -1)
    states, linkage, cumulative = span_states(
        inner_act, input_mat, step_size, decay_rate, seg_part, seg_before
    )
    incoming = entering(
        (linkage, states),
        "ctx",
        combine_state,
        (jnp.ones_like(linkage), jnp.zeros_like(states)),
        False,
    )[1]

    def local_mixer(inner_arg, input_arg, output_arg, step_arg, rate_arg):
        states_new, linkage_new, cumulative_new = span_states(
            inner_arg, input_arg, step_arg, rate_arg, seg_part, seg_before
        )
        result = span_outputs(
            inner_arg,
            input_arg,
            output_arg,
            step_arg,
            seg_part,
            seg_before,
            cumulative_new,
            incoming,
        )
        return (result, states_new, linkage_new)

    mixer_values, mixer_pull = jax.vjp(
        local_mixer, inner_act, input_mat, output_mat, step_size, decay_rate
    )
    ssm_flat = mixer_values[0].reshape(row_count, inner_width)
    gated = (ssm_flat * jax.nn.silu(gate_lin)).astype(jnp.bfloat16)
    cos_table, sin_table = rotary_tables(offset + jnp.arange(span_len), head_dim)
    rotated_q = rotate(
        queries.reshape(seq_count, span_len, query_heads, head_dim),
        cos_table[:, None],
        sin_table[:, None],
    ).astype(jnp.bfloat16)
    keyval_seq = keyval.reshape(seq_count, span_len, 2 * head_dim)
    keyval_low = jnp.concatenate(
        [rotate(keyval_seq[..., :head_dim], cos_table, sin_table), keyval_seq[..., head_dim:]],
        axis=-1,
    ).astype(jnp.bfloat16)
    all_keys = fetch_keys(keyval_low)

    def forward_one(sequence):
        return attend_forward(sequence[0], sequence[1], sequence[2], sequence[3], offset)

    attended, log_total = lax.map(forward_one, (rotated_q, all_keys, segments, seg_part))
    attended_low = attended.reshape(row_count, query_width).astype(jnp.bfloat16)
    mixer_sum = lax.psum(
        (matmul(gated, full_mixout) + matmul(attended_low, full_attnout)).astype(jnp.bfloat16), "tp"
    ).astype(jnp.float32)
    hidden = inputs + mixer_sum
    inv_rms_ffn = lax.rsqrt(jnp.mean(hidden * hidden, axis=1, keepdims=True) + epsilon)
    normed_ffn = (hidden * inv_rms_ffn * ffn_gain).astype(jnp.bfloat16)
    gate_ffn = matmul(normed_ffn, full_ffngate)
    up_ffn = matmul(normed_ffn, full_ffnup)
    act_ffn = (jax.nn.silu(gate_ffn) * up_ffn).astype(jnp.bfloat16)
    ffn_result = lax.psum(matmul(act_ffn, full_ffndown).astype(jnp.bfloat16), "tp").astype(
        jnp.float32
    )
    layer_out = (hidden + ffn_result).astype(jnp.bfloat16).reshape(seq_count, span_len, model_width)
    weights_back = fetch_weights(
        ssm_gate,
        ssm_input,
        ssm_state,
        ssm_step,
        attn_query,
        attn_keyval,
        ssm_out,
        attn_out,
        ffn_gate,
        ffn_up,
        ffn_down,
    )
    (
        back_gate,
        back_input,
        back_state,
        back_step,
        back_query,
        back_keyval,
        back_mixout,
        back_attnout,
        back_ffngate,
        back_ffnup,
        back_ffndown,
    ) = weights_back
    back_keyval_flat = back_keyval.reshape(model_width, 2 * head_dim)
    grad_out = cotangent.reshape(row_count, model_width)
    grad_act = back_product(grad_out, back_ffndown)
    grad_ffndown = weight_grad(act_ffn, grad_out)
    sig_gate = jax.nn.sigmoid(gate_ffn)
    grad_up = (grad_act * gate_ffn * sig_gate).astype(jnp.bfloat16)
    grad_gate = (grad_act * up_ffn * sig_gate * (1.0 + gate_ffn * (1.0 - sig_gate))).astype(
        jnp.bfloat16
    )
    grad_ffngate = weight_grad(normed_ffn, grad_gate)
    grad_ffnup = weight_grad(normed_ffn, grad_up)
    grad_normed_ffn = lax.psum(
        (back_product(grad_gate, back_ffngate) + back_product(grad_up, back_ffnup)).astype(
            jnp.bfloat16
        ),
        "tp",
    ).astype(jnp.float32)
    grad_ffn_gain = jnp.sum(grad_normed_ffn * hidden * inv_rms_ffn, axis=0)
    scaled_ffn = grad_normed_ffn * ffn_gain
    grad_hidden = (
        grad_out.astype(jnp.float32)
        + inv_rms_ffn * scaled_ffn
        - hidden * inv_rms_ffn**3 * jnp.mean(scaled_ffn * hidden, axis=1, keepdims=True)
    )
    grad_hidden_low = grad_hidden.astype(jnp.bfloat16)
    grad_mixout = weight_grad(gated, grad_hidden_low)
    grad_attnout = weight_grad(attended_low, grad_hidden_low)
    grad_gated = back_product(grad_hidden_low, back_mixout)
    grad_attended = (
        back_product(grad_hidden_low, back_attnout)
        .astype(jnp.bfloat16)
        .reshape(seq_count, span_len, query_heads, head_dim)
    )
    sig_zeta = jax.nn.sigmoid(gate_lin)
    grad_ssm = (grad_gated * gate_lin * sig_zeta).reshape(
        seq_count, span_len, local_heads, head_size
    )
    grad_zeta = (grad_gated * ssm_flat * sig_zeta * (1.0 + gate_lin * (1.0 - sig_zeta))).astype(
        jnp.bfloat16
    )
    entrance = jnp.where((seg_part == seg_before[:, None])[..., None], jnp.exp(cumulative), 0.0)
    local_grad = jnp.einsum(
        "stha,stn->shan", grad_ssm * entrance[..., None], output_mat, precision=highest
    )
    later_grad = entering(
        (linkage, local_grad),
        "ctx",
        combine_state,
        (jnp.ones_like(linkage), jnp.zeros_like(local_grad)),
        True,
    )[1]
    grad_link = jnp.sum(later_grad * incoming, axis=(2, 3))
    grad_inner, grad_input_mat, grad_output_mat, grad_step, grad_decay_rate = mixer_pull(
        (grad_ssm, later_grad, grad_link)
    )
    grad_step_lin = grad_step.reshape(row_count, local_heads) * jax.nn.sigmoid(step_lin + step_bias)
    grad_step_bias = jnp.sum(grad_step_lin, axis=0)
    grad_step_low = grad_step_lin.astype(jnp.bfloat16)
    grad_activated = jnp.concatenate(
        [grad_inner.reshape(seq_count, span_len, inner_width), grad_input_mat, grad_output_mat],
        axis=2,
    )
    sig_conv = jax.nn.sigmoid(conv_sum)
    grad_conv = grad_activated * sig_conv * (1.0 + conv_sum * (1.0 - sig_conv))
    grad_taps_inner, grad_pad_inner = conv_back(
        grad_conv[..., :inner_width], padded[..., :inner_width], conv_input
    )
    rim_inner = shifted(grad_pad_inner[:, : tap_count - 1].astype(jnp.bfloat16), "ctx", -1).astype(
        jnp.float32
    )
    grad_mixer_inner = (
        add_rim(grad_pad_inner, rim_inner, tap_count)
        .astype(jnp.bfloat16)
        .reshape(row_count, inner_width)
    )
    keys_back = fetch_keys(keyval_low)

    def backward_one(sequence):
        return attend_backward(
            sequence[0], sequence[1], sequence[2], sequence[3], sequence[4], sequence[5], offset
        )

    grad_rot_q, grad_keyval_all = lax.map(
        backward_one, (rotated_q, keys_back, segments, seg_part, log_total, grad_attended)
    )
    grad_keyval_rot = lax.psum_scatter(
        grad_keyval_all.astype(jnp.bfloat16), "ctx", scatter_dimension=1, tiled=True
    ).astype(jnp.float32)
    grad_queries = (
        rotate_back(grad_rot_q, cos_table[:, None], sin_table[:, None])
        .reshape(row_count, query_width)
        .astype(jnp.bfloat16)
    )
    grad_keyval_low = jnp.concatenate(
        [
            rotate_back(grad_keyval_rot[..., :head_dim], cos_table, sin_table),
            grad_keyval_rot[..., head_dim:],
        ],
        axis=-1,
    )
    grad_keyval_low = grad_keyval_low.reshape(row_count, 2 * head_dim).astype(jnp.bfloat16)
    grad_norm_part = (
        back_product(grad_zeta, back_gate)
        + back_product(grad_mixer_inner, back_input)
        + back_product(grad_step_low, back_step)
        + back_product(grad_queries, back_query)
        + back_product(grad_keyval_low, back_keyval_flat)
    )
    grad_norm_sum, grad_conv_state = (
        lax.psum(grad_norm_part.astype(jnp.bfloat16), "tp").astype(jnp.float32),
        lax.psum(grad_conv[..., inner_width:].astype(jnp.bfloat16), "tp").astype(jnp.float32),
    )
    grad_taps_state, grad_pad_state = conv_back(
        grad_conv_state, padded[..., inner_width:], conv_state
    )
    rim_state = shifted(grad_pad_state[:, : tap_count - 1], "ctx", -1)
    grad_mixer_state = (
        add_rim(grad_pad_state, rim_state, tap_count)
        .astype(jnp.bfloat16)
        .reshape(row_count, 2 * state_width)
    )
    grad_normed = grad_norm_sum + back_product(grad_mixer_state, back_state)
    grad_mix_gain = jnp.sum(grad_normed * inputs * inv_rms, axis=0)
    scaled_mix = grad_normed * mix_gain
    grad_tokens = (
        grad_hidden
        + inv_rms * scaled_mix
        - inputs * inv_rms**3 * jnp.mean(scaled_mix * inputs, axis=1, keepdims=True)
    )
    grad_gate_w = weight_grad(normed, grad_zeta)
    grad_input_w = weight_grad(normed, grad_mixer_inner)
    grad_state_w = weight_grad(normed, grad_mixer_state)
    grad_step_w = weight_grad(normed, grad_step_low)
    grad_query_w = weight_grad(normed, grad_queries)
    grad_keyval_w = weight_grad(normed, grad_keyval_low).reshape(model_width, 1, 2 * head_dim)
    summed = (
        lax.psum_scatter(grad_gate_w, ("shard", "ctx"), scatter_dimension=0, tiled=True),
        lax.psum_scatter(grad_input_w, ("shard", "ctx"), scatter_dimension=0, tiled=True),
        lax.psum_scatter(grad_state_w, ("shard", "ctx"), scatter_dimension=0, tiled=True),
        lax.psum_scatter(grad_step_w, ("shard", "ctx"), scatter_dimension=0, tiled=True),
        lax.psum_scatter(grad_query_w, ("shard", "ctx"), scatter_dimension=0, tiled=True),
        lax.psum_scatter(grad_keyval_w, ("shard", "ctx"), scatter_dimension=0, tiled=True),
        lax.psum_scatter(grad_mixout, ("shard", "ctx"), scatter_dimension=1, tiled=True),
        lax.psum_scatter(grad_attnout, ("shard", "ctx"), scatter_dimension=1, tiled=True),
        lax.psum_scatter(grad_ffngate, ("shard", "ctx"), scatter_dimension=0, tiled=True),
        lax.psum_scatter(grad_ffnup, ("shard", "ctx"), scatter_dimension=0, tiled=True),
        lax.psum_scatter(grad_ffndown, ("shard", "ctx"), scatter_dimension=1, tiled=True),
    )
    small_sums = lax.psum(
        (
            grad_taps_inner,
            grad_taps_state,
            grad_step_bias,
            grad_decay_rate,
            grad_mix_gain,
            grad_ffn_gain,
        ),
        ("shard", "ctx"),
    )
    return (
        layer_out,
        grad_tokens.reshape(seq_count, span_len, model_width),
        small_sums[4],
        small_sums[5],
        summed[0],
        summed[1],
        summed[2],
        summed[3],
        summed[4],
        summed[5],
        summed[6],
        summed[7],
        summed[8],
        summed[9],
        summed[10],
        small_sums[0],
        small_sums[1],
        small_sums[2],
        small_sums[3],
    )


def solution(mesh):
    in_specs = (
        P("shard", "ctx", None),
        P("shard", None),
        P("shard", "ctx", None),
        P(),
        P(),
        P(("shard", "ctx"), "tp"),
        P(("shard", "ctx"), "tp"),
        P(("shard", "ctx"), None),
        P(("shard", "ctx"), "tp"),
        P(("shard", "ctx"), "tp"),
        P(("shard", "ctx"), "tp", None),
        P("tp", ("shard", "ctx")),
        P("tp", ("shard", "ctx")),
        P(("shard", "ctx"), "tp"),
        P(("shard", "ctx"), "tp"),
        P("tp", ("shard", "ctx")),
        P(None, "tp"),
        P(),
        P("tp"),
        P("tp"),
    )
    out_specs = (
        P("shard", "ctx", None),
        P("shard", "ctx", None),
        P(),
        P(),
        P(("shard", "ctx"), "tp"),
        P(("shard", "ctx"), "tp"),
        P(("shard", "ctx"), None),
        P(("shard", "ctx"), "tp"),
        P(("shard", "ctx"), "tp"),
        P(("shard", "ctx"), "tp", None),
        P("tp", ("shard", "ctx")),
        P("tp", ("shard", "ctx")),
        P(("shard", "ctx"), "tp"),
        P(("shard", "ctx"), "tp"),
        P("tp", ("shard", "ctx")),
        P(None, "tp"),
        P(),
        P("tp"),
        P("tp"),
    )
    return jax.shard_map(shards, mesh=mesh, in_specs=in_specs, out_specs=out_specs, check_vma=False)
```

profile of v0, /device:TPU:0, one launch (start us, length us, event | category | flops | bytes accessed | tf_op | source)
XLA Modules:
  0.0 1951.8 jit_solution(2665427767071738628)
XLA Ops:
  16.9 42.8 %all-gather.2 = bf16[16,64,12]{1,2,0:T(8,128)(2,1)S(1)} all-gather(bf16[1,64,12]{1,2,0:T(8,128)(2,1)S(1)} %bitcast.557), channel_id=1, replica_groups=mesh['shard'=8,'ctx'=2,'tp'=2] {'shard','ctx'}, dimensions={0}, use_global_device_ids=true | all-gather | bytes 26112 | tf_op jit(solution)/shard_map/all_gather | solution.py:219
  59.9 37.3 %all_gather.74 = bf16[1024,1,128]{2,0,1:T(8,128)(2,1)S(1)} all-gather(bf16[64,1,128]{2,0,1:T(8,128)(2,1)S(1)} %copy-done.104), channel_id=1, replica_groups=mesh['shard'=8,'ctx'=2,'tp'=2] {'shard','ctx'}, dimensions={0}, use_global_device_ids=true | all-gather | bytes 278528 | tf_op jit(solution)/shard_map/all_gather | solution.py:221
  98.5 41.8 %all_gather.67 = bf16[1024,256]{1,0:T(8,128)(2,1)S(1)} all-gather(bf16[64,256]{1,0:T(8,128)(2,1)S(1)} %copy-done.93), channel_id=1, replica_groups=mesh['shard'=8,'ctx'=2,'tp'=2] {'shard','ctx'}, dimensions={0}, use_global_device_ids=true | all-gather | bytes 557056 | tf_op jit(solution)/shard_map/all_gather | solution.py:218
  140.3 40.8 %all_gather.76 = bf16[1024,256]{1,0:T(8,128)(2,1)S(1)} all-gather(bf16[64,256]{1,0:T(8,128)(2,1)} %param.37), channel_id=1, replica_groups=mesh['shard'=8,'ctx'=2,'tp'=2] {'shard','ctx'}, dimensions={0}, use_global_device_ids=true | all-gather | bytes 557056 | tf_op jit(solution)/shard_map/all_gather | solution.py:220
  181.1 42.8 %all_gather.77 = bf16[256,1024]{0,1:T(8,128)(2,1)} all-gather(bf16[256,64]{0,1:T(8,128)(2,1)} %param.40), channel_id=1, replica_groups=mesh['shard'=8,'ctx'=2,'tp'=2] {'shard','ctx'}, dimensions={1}, use_global_device_ids=true | all-gather | bytes 557056 | tf_op jit(solution)/shard_map/all_gather | solution.py:223
  226.8 7.3 all_gather.75
  236.7 14.1 while.58
  293.1 8.6 all-gather
  313.3 29.9 %bitcast_add_fusion.2 = f32[2,512,12,64]{1,3,2,0:T(8,128)S(1)} fusion(f32[2,512,12,64]{1,3,2,0:T(8,128)S(1)} %fusion.130, f32[2,512,12,64]{1,3,2,0:T(8,128)S(1)} %bitcast.499, f32[2,512,12]{1,2,0:T(8,128)S(1)} %copy-done.77, f32[2,512,12]{1,2,0:T(8,128)S(1)} %bitcast.522, f32[2,512,512]{2,1,0:T(8,128)S(1)} %fusion.139, ...), kind=kOutput, calls=%fused_computation.158 | convolution fusion | flops 4864868352 | bytes 12206080 | tf_op jit(solution)/shard_map/jvp(stuh,suha->stha)/dot_general | solution.py:113
  351.6 7.2 multiply_convert_fusion.5
  367.1 15.2 all-reduce.16.cloned.1.call-done
  387.4 59.6 %all-gather.18.cloned.1.call-done = bf16[1024,1024]{1,0:T(8,128)(2,1)} async-done(((bf16[64,1024]{1,0:T(8,128)(2,1)}), bf16[1024,1024]{1,0:T(8,128)(2,1)}) %all-gather.18.cloned.1.call-update) | async-done | bytes 2097168 | tf_op jit(solution)/shard_map/all_gather | solution.py:225
  447.0 6.5 fusion.183
  453.5 55.8 %all-gather.16.cloned.1.call-done = bf16[1024,1024]{1,0:T(8,128)(2,1)} async-done(((bf16[64,1024]{1,0:T(8,128)(2,1)}), bf16[1024,1024]{1,0:T(8,128)(2,1)}) %all-gather.16.cloned.1.call-update) | async-done | bytes 2097168 | tf_op jit(solution)/shard_map/all_gather | solution.py:224
  509.3 6.6 fusion.182
  515.9 55.8 %all-gather.20.cloned.1.call-done = bf16[1024,1024]{0,1:T(8,128)(2,1)} async-done(((bf16[1024,64]{0,1:T(8,128)(2,1)}), bf16[1024,1024]{0,1:T(8,128)(2,1)}) %all-gather.20.cloned.1.call-update) | async-done | bytes 2097168 | tf_op jit(solution)/shard_map/all_gather | solution.py:226
  571.8 10.0 multiply_convert_fusion
  590.3 5.9 convolution_convert_fusion
  596.3 12.5 all-reduce.18.cloned.1.call-done
  627.2 5.8 reshape.685
  641.7 6.0 fusion.121
  647.8 12.0 all-gather.1
  660.8 7.9 fusion.122
  668.7 6.3 multiply_reduce_fusion.3
  676.9 26.2 %while.59 = (s32[]{:T(128)}, f32[2,512,4,64]{1,3,2,0:T(8,128)}, bf16[2,1024,128]{1,2,0:T(8,128)(2,1)}, bf16[2,1024,128]{1,2,0:T(8,128)(2,1)S(1)}, s32[]{:T(128)}...) while((s32[]{:T(128)}, f32[2,512,4,64]{1,3,2,0:T(8,128)}, ...), condition=%wide.region_28.29_spmd.clone, body=%wide.region_26.28_spmd.sunk.clone | while | flops 1375992320 | bytes 76757192 | solution.py:490
  706.2 40.4 %fusion.56 = (f32[2,512,12]{1,2,0:T(8,128)}, f32[2,512,12]{1,2,0:T(8,128)}, f32[2,512,12]{1,2,0:T(8,128)}, f32[2,512,512]{2,1,0:T(8,128)S(1)}) fusion(f32[2,512,12]{1,2,0:T(8,128)} %get-tuple-element.627, f32[2,512,12]{1,2,0:T(8,128)S(1)} %bitcast.524, f32[2,512,512]{2,1,0:T(8,128)S(1)} %copy-done.41, pred[2,512,512]{2,1,0:T(8,128)(4,1)} %compare_and_fusion, ...), kind=kOutput, calls=%fused_computation.86 | convolution fusion | flops 4925648896 | bytes 11255808 | tf_op jit(solution)/shard_map/transpose(jvp(stuh,suha->stha))/dot_general | solution.py:113
  746.6 25.3 %bitcast_add_fusion.1 = f32[2,512,12,64]{1,3,2,0:T(8,128)} fusion(f32[2,512,12,64]{1,3,2,0:T(8,128)S(1)} %copy-done.33, f32[2,512,12]{1,2,0:T(8,128)S(1)} %copy-done.78, f32[2,512,12]{1,2,0:T(8,128)S(1)} %bitcast.525, f32[2,512,512]{2,1,0:T(8,128)S(1)} %copy-done.41, pred[2,512,512]{2,1,0:T(8,128)(4,1)S(1)} %copy-done.61, ...), kind=kOutput, calls=%fused_computation.157 | convolution fusion | flops 4864868352 | bytes 12206080 | tf_op jit(solution)/shard_map/transpose(jvp(stuh,suha->stha))/dot_general | solution.py:113
  775.8 5.4 convolution_add_fusion.1
  785.3 9.9 reduce-window.16
  806.5 5.3 fusion.185
  822.6 6.8 add_convert_fusion
  840.0 7.6 fusion.193
  847.9 5.5 fusion.189
  853.5 7.0 fusion.191
  860.6 6.5 fusion.192
  867.2 5.6 fusion.187
  889.7 51.7 %reduce-scatter.37.cloned.1.call-done = f32[64,12]{1,0:T(8,128)} async-done(((f32[1024,12]{1,0:T(8,128)}), f32[64,12]{1,0:T(8,128)}) %reduce-scatter.37.cloned.1.call-update) | async-done | bytes 3088
  948.0 72.1 %all-reduce.10 = (f32[1024]{0:T(1024)}, f32[1024]{0:T(1024)}, f32[4,768]{1,0:T(4,128)}, f32[4,256]{1,0:T(4,128)}, f32[12]{0:T(128)}, /*index=5*/f32[12]{0:T(128)}) all-reduce(f32[1024]{0:T(1024)S(1)} %get-tuple-element.509, f32[1024]{0:T(1024)S(1)} %copy-done.99, ...), channel_id=1, replica_groups=mesh['shard'=8,'ctx'=2,'tp'=2] {'shard','ctx'}, use_global_device_ids=true, to_apply=%region_34.35 | all-reduce | flops 6168 | bytes 49344 | tf_op jit(solution)/shard_map/psum | solution.py:556
  1020.2 7.9 fusion.86
  1028.1 66.0 %reduce-scatter.29.cloned.1.call-done = f32[256,64]{0,1:T(8,128)} async-done(((f32[256,1024]{0,1:T(8,128)}), f32[256,64]{0,1:T(8,128)}) %reduce-scatter.29.cloned.1.call-update) | async-done | bytes 65552 | tf_op jit(solution)/shard_map/reduce_scatter | solution.py:551
  1094.1 77.0 %reduce-scatter.23.cloned.1.call-done = f32[64,256]{1,0:T(8,128)} async-done(((f32[1024,256]{1,0:T(8,128)}), f32[64,256]{1,0:T(8,128)}) %reduce-scatter.23.cloned.1.call-update) | async-done | bytes 65552 | tf_op jit(solution)/shard_map/reduce_scatter | solution.py:548
  1171.1 94.8 %reduce-scatter.35.cloned.1.call-done = f32[1024,64]{0,1:T(8,128)} async-done(((f32[1024,1024]{0,1:T(8,128)}), f32[1024,64]{0,1:T(8,128)}) %reduce-scatter.35.cloned.1.call-update) | async-done | bytes 262160 | tf_op jit(solution)/shard_map/reduce_scatter | solution.py:554
  1265.8 134.5 %reduce-scatter.27.cloned.1.call-done = f32[768,64]{0,1:T(8,128)} async-done(((f32[768,1024]{0,1:T(8,128)}), f32[768,64]{0,1:T(8,128)}) %reduce-scatter.27.cloned.1.call-update) | async-done | bytes 196624 | tf_op jit(solution)/shard_map/reduce_scatter | solution.py:550
  1400.3 97.7 %reduce-scatter.31.cloned.1.call-done = f32[64,1024]{1,0:T(8,128)} async-done(((f32[1024,1024]{1,0:T(8,128)}), f32[64,1024]{1,0:T(8,128)}) %reduce-scatter.31.cloned.1.call-update) | async-done | bytes 262160 | tf_op jit(solution)/shard_map/reduce_scatter | solution.py:552
  1498.0 96.5 %reduce-scatter.33.cloned.1.call-done = f32[64,1024]{1,0:T(8,128)} async-done(((f32[1024,1024]{1,0:T(8,128)}), f32[64,1024]{1,0:T(8,128)}) %reduce-scatter.33.cloned.1.call-update) | async-done | bytes 262160 | tf_op jit(solution)/shard_map/reduce_scatter | solution.py:553
  1594.5 134.9 %reduce-scatter.17.cloned.1.call-done = f32[64,768]{1,0:T(8,128)} async-done(((f32[1024,768]{1,0:T(8,128)}), f32[64,768]{1,0:T(8,128)}) %reduce-scatter.17.cloned.1.call-update) | async-done | bytes 196624 | tf_op jit(solution)/shard_map/reduce_scatter | solution.py:544
  1729.3 135.4 %reduce-scatter.19.cloned.1.call-done = f32[64,768]{1,0:T(8,128)} async-done(((f32[1024,768]{1,0:T(8,128)}), f32[64,768]{1,0:T(8,128)}) %reduce-scatter.19.cloned.1.call-update) | async-done | bytes 196624 | tf_op jit(solution)/shard_map/reduce_scatter | solution.py:545
  1864.8 79.9 %reduce-scatter.21.cloned.1.call-done = f32[64,256]{1,0:T(8,128)} async-done(((f32[1024,256]{1,0:T(8,128)}), f32[64,256]{1,0:T(8,128)}) %reduce-scatter.21.cloned.1.call-update) | async-done | bytes 65552 | tf_op jit(solution)/shard_map/reduce_scatter | solution.py:546
  (519 shorter events, 239.4 us)
Async XLA Ops:
  7.2 52.6 %copy-start.104 = (bf16[64,1,128]{2,0,1:T(8,128)(2,1)S(1)}, bf16[64,1,128]{2,0,1:T(8,128)(2,1)}, u32[]{:S(2)}) copy-start(bf16[64,1,128]{2,0,1:T(8,128)(2,1)} %param.38) | copy-start | bytes 49156
  7.2 91.2 %copy-start.93 = (bf16[64,256]{1,0:T(8,128)(2,1)S(1)}, bf16[64,256]{1,0:T(8,128)(2,1)}, u32[]{:S(2)}) copy-start(bf16[64,256]{1,0:T(8,128)(2,1)} %param.35) | copy-start | bytes 98308
  7.2 250.7 %all-gather.10.cloned.1.call-start = ((), (), s32[]{:S(2)}) async-start(), calls=%async_computation.12 | async-start | bytes 1671168 | tf_op jit(solution)/shard_map/all_gather | solution.py:217
  8.0 343.6 %all-gather.12.cloned.1.call-start = ((), (), s32[]{:S(2)}) async-start(), calls=%async_computation.13 | async-start | bytes 1671168 | tf_op jit(solution)/shard_map/all_gather | solution.py:216
  8.7 350.0 %all-gather.14.cloned.1.call-start = ((), (), s32[]{:S(2)}) async-start(), calls=%async_computation.14 | async-start | bytes 1671168 | tf_op jit(solution)/shard_map/all_gather | solution.py:222
  9.5 372.8 %all-reduce.16.cloned.1.call-start = ((), (), s32[]{:S(2)}) async-start(), calls=%async_computation.15 | async-start | bytes 4194304 | tf_op jit(solution)/shard_map/psum | solution.py:369
  13.3 211.6 %copy-start.1 = (bf16[2,512,1024]{2,1,0:T(8,128)(2,1)S(1)}, bf16[2,512,1024]{2,1,0:T(8,128)(2,1)}, u32[]{:S(2)}) copy-start(bf16[2,512,1024]{2,1,0:T(8,128)(2,1)} %param.28) | copy-start | bytes 6291460
  13.3 211.6 %copy-start.90 = (f32[1024]{0:T(1024)S(1)}, f32[1024]{0:T(1024)}, u32[]{:S(2)}) copy-start(f32[1024]{0:T(1024)} %param.31) | copy-start | bytes 12292
  15.6 235.3 %copy-start.80 = (f32[1,4,2,128]{3,1,2,0:T(4,128)}, f32[1,4,2,128]{3,1,2,0:T(4,128)S(1)}, u32[]{:S(2)}) copy-start(f32[1,4,2,128]{3,1,2,0:T(4,128)S(1)} %copy.268) | copy-start | bytes 12292
  59.8 191.6 %copy-start.65 = (bf16[1024,12]{0,1:T(8,128)(2,1)}, bf16[1024,12]{0,1:T(8,128)(2,1)S(1)}, u32[]{:S(2)}) copy-start(bf16[1024,12]{0,1:T(8,128)(2,1)S(1)} %reshape.702) | copy-start | bytes 73732
  97.1 128.4 %copy-start.34 = (bf16[1024,1,128]{2,0,1:T(8,128)(2,1)}, bf16[1024,1,128]{2,0,1:T(8,128)(2,1)S(1)}, u32[]{:S(2)}) copy-start(bf16[1024,1,128]{2,0,1:T(8,128)(2,1)S(1)} %all_gather.74) | copy-start | bytes 786436
  97.2 160.0 %copy-start.82 = (pred[2,512]{1,0:T(4,128)(4,1)}, pred[2,512]{1,0:T(4,128)(4,1)S(1)}, u32[]{:S(2)}) copy-start(pred[2,512]{1,0:T(4,128)(4,1)S(1)} %broadcast_compare_fusion.1) | copy-start | bytes 3076
  140.3 93.9 %copy-start.62 = (bf16[1024,256]{1,0:T(8,128)(2,1)}, bf16[1024,256]{1,0:T(8,128)(2,1)S(1)}, u32[]{:S(2)}) copy-start(bf16[1024,256]{1,0:T(8,128)(2,1)S(1)} %all_gather.67) | copy-start | bytes 1572868
  181.1 45.2 %copy-start.30 = (bf16[1024,256]{1,0:T(8,128)(2,1)}, bf16[1024,256]{1,0:T(8,128)(2,1)S(1)}, u32[]{:S(2)}) copy-start(bf16[1024,256]{1,0:T(8,128)(2,1)S(1)} %all_gather.76) | copy-start | bytes 1572868
  257.9 402.9 %copy-start.55 = (f32[2,512,12]{1,2,0:T(8,128)}, f32[2,512,12]{1,2,0:T(8,128)S(1)}, u32[]{:S(2)}) copy-start(f32[2,512,12]{1,2,0:T(8,128)S(1)} %get-tuple-element.626) | copy-start | bytes 147460
  263.6 11.6 collective-permute-start
  364.7 82.3 %all-gather.18.cloned.1.call-start = ((), (), s32[]{:S(2)}) async-start(), calls=%async_computation.17 | async-start | bytes 2228224 | tf_op jit(solution)/shard_map/all_gather | solution.py:225
  365.3 144.0 %all-gather.16.cloned.1.call-start = ((), (), s32[]{:S(2)}) async-start(), calls=%async_computation.16 | async-start | bytes 2228224 | tf_op jit(solution)/shard_map/all_gather | solution.py:224
  365.9 205.9 %all-gather.20.cloned.1.call-start = ((), (), s32[]{:S(2)}) async-start(), calls=%async_computation.18 | async-start | bytes 2228224 | tf_op jit(solution)/shard_map/all_gather | solution.py:226
  366.6 242.2 %all-reduce.18.cloned.1.call-start = ((), (), s32[]{:S(2)}) async-start(), calls=%async_computation.19 | async-start | bytes 4194304 | tf_op jit(solution)/shard_map/psum | solution.py:419
  385.3 228.2 %copy-start.70 = (f32[1024]{0:T(1024)}, f32[1024]{0:T(1024)S(1)}, u32[]{:S(2)}) copy-start(f32[1024]{0:T(1024)S(1)} %get-tuple-element.637) | copy-start | bytes 12292
  588.8 230.0 %reduce-scatter.15.cloned.1.call-start = ((), (), s32[]{:S(2)}) async-start(), calls=%async_computation.20 | async-start | bytes 786432 | tf_op jit(solution)/shard_map/reduce_scatter | solution.py:493
  703.1 175.4 %all-reduce.20.cloned.1.call-start = ((), (), s32[]{:S(2)}) async-start(), calls=%async_computation.32 | async-start | bytes 9437184 | tf_op jit(solution)/shard_map/psum | solution.py:378
  706.1 40.5 %copy-start.12 = (f32[2,512,12,64]{1,0,3,2:T(2,128)S(1)}, f32[2,512,12,64]{1,0,3,2:T(2,128)}, u32[]{:S(2)}) copy-start(f32[2,512,12,64]{1,0,3,2:T(2,128)} %reshape.685) | copy-start | bytes 9437188
  706.1 40.5 %copy-start.33 = (f32[2,512,12,64]{1,3,2,0:T(8,128)S(1)}, f32[2,512,12,64]{1,3,2,0:T(8,128)}, u32[]{:S(2)}) copy-start(f32[2,512,12,64]{1,3,2,0:T(8,128)} %get-tuple-element.647) | copy-start | bytes 9437188
  706.1 40.5 %copy-start.56 = (f32[2,512,12]{1,2,0:T(8,128)S(1)}, f32[2,512,12]{1,2,0:T(8,128)}, u32[]{:S(2)}) copy-start(f32[2,512,12]{1,2,0:T(8,128)} %copy-done.55) | copy-start | bytes 147460
  706.2 40.4 %copy-start.61 = (pred[2,512,512]{2,1,0:T(8,128)(4,1)S(1)}, pred[2,512,512]{2,1,0:T(8,128)(4,1)}, u32[]{:S(2)}) copy-start(pred[2,512,512]{2,1,0:T(8,128)(4,1)} %compare_and_fusion) | copy-start | bytes 1572868
  706.2 40.4 %copy-start.78 = (f32[2,512,12]{1,2,0:T(8,128)S(1)}, f32[2,512,12]{1,2,0:T(8,128)}, u32[]{:S(2)}) copy-start(f32[2,512,12]{1,2,0:T(8,128)} %get-tuple-element.627) | copy-start | bytes 147460
  804.8 13.7 collective-permute-start.1
  829.5 111.9 %reduce-scatter.37.cloned.1.call-start = ((), (), s32[]{:S(2)}) async-start(), calls=%async_computation.31 | async-start | bytes 557056
  832.9 195.2 %reduce-scatter.25.cloned.1.call-start = ((), (), s32[]{:S(2)}) async-start(), calls=%async_computation.25 | async-start | bytes 557056 | tf_op jit(solution)/shard_map/reduce_scatter | solution.py:549
  834.5 259.6 %reduce-scatter.29.cloned.1.call-start = ((), (), s32[]{:S(2)}) async-start(), calls=%async_computation.27 | async-start | bytes 1114112 | tf_op jit(solution)/shard_map/reduce_scatter | solution.py:551
  838.1 333.0 %reduce-scatter.23.cloned.1.call-start = ((), (), s32[]{:S(2)}) async-start(), calls=%async_computation.24 | async-start | bytes 1114112 | tf_op jit(solution)/shard_map/reduce_scatter | solution.py:548
  840.0 425.8 %reduce-scatter.35.cloned.1.call-start = ((), (), s32[]{:S(2)}) async-start(), calls=%async_computation.30 | async-start | bytes 4456448 | tf_op jit(solution)/shard_map/reduce_scatter | solution.py:554
  847.6 552.7 %reduce-scatter.27.cloned.1.call-start = ((), (), s32[]{:S(2)}) async-start(), calls=%async_computation.26 | async-start | bytes 3342336 | tf_op jit(solution)/shard_map/reduce_scatter | solution.py:550
  853.5 644.5 %reduce-scatter.31.cloned.1.call-start = ((), (), s32[]{:S(2)}) async-start(), calls=%async_computation.28 | async-start | bytes 4456448 | tf_op jit(solution)/shard_map/reduce_scatter | solution.py:552
  860.5 733.9 %reduce-scatter.33.cloned.1.call-start = ((), (), s32[]{:S(2)}) async-start(), calls=%async_computation.29 | async-start | bytes 4456448 | tf_op jit(solution)/shard_map/reduce_scatter | solution.py:553
  867.2 862.2 %reduce-scatter.17.cloned.1.call-start = ((), (), s32[]{:S(2)}) async-start(), calls=%async_computation.21 | async-start | bytes 3342336 | tf_op jit(solution)/shard_map/reduce_scatter | solution.py:544
  872.8 992.0 %reduce-scatter.19.cloned.1.call-start = ((), (), s32[]{:S(2)}) async-start(), calls=%async_computation.22 | async-start | bytes 3342336 | tf_op jit(solution)/shard_map/reduce_scatter | solution.py:545
  877.9 1066.8 %reduce-scatter.21.cloned.1.call-start = ((), (), s32[]{:S(2)}) async-start(), calls=%async_computation.23 | async-start | bytes 1114112 | tf_op jit(solution)/shard_map/reduce_scatter | solution.py:546
  882.2 5.5 collective-permute-start.2
  887.8 55.0 %copy-start.2 = (bf16[2,512,1024]{2,1,0:T(8,128)(2,1)S(1)}, bf16[2,512,1024]{2,1,0:T(8,128)(2,1)}, u32[]{:S(2)}) copy-start(bf16[2,512,1024]{2,1,0:T(8,128)(2,1)} %param.28) | copy-start | bytes 6291460
  887.8 55.0 %copy-start.63 = (bf16[1024,256]{1,0:T(8,128)(2,1)S(1)}, bf16[1024,256]{1,0:T(8,128)(2,1)}, u32[]{:S(2)}) copy-start(bf16[1024,256]{1,0:T(8,128)(2,1)} %copy-done.62) | copy-start | bytes 1572868
  887.8 55.0 %copy-start.92 = (f32[1024]{0:T(1024)S(1)}, f32[1024]{0:T(1024)}, u32[]{:S(2)}) copy-start(f32[1024]{0:T(1024)} %param.31) | copy-start | bytes 12292
  942.9 77.3 %copy-start.71 = (f32[1024]{0:T(1024)S(1)}, f32[1024]{0:T(1024)}, u32[]{:S(2)}) copy-start(f32[1024]{0:T(1024)} %copy-done.70) | copy-start | bytes 12292
  942.9 77.2 %copy-start.76 = (f32[1024]{0:T(1024)S(1)}, f32[1024]{0:T(1024)}, u32[]{:S(2)}) copy-start(f32[1024]{0:T(1024)} %param.32) | copy-start | bytes 12292
  942.9 77.2 %copy-start.87 = (f32[1024]{0:T(1024)S(1)}, f32[1024]{0:T(1024)}, u32[]{:S(2)}) copy-start(f32[1024]{0:T(1024)} %get-tuple-element.636) | copy-start | bytes 12292
  942.9 77.2 %copy-start.89 = (f32[1024]{0:T(1024)S(1)}, f32[1024]{0:T(1024)}, u32[]{:S(2)}) copy-start(f32[1024]{0:T(1024)} %copy-done.88) | copy-start | bytes 12292
  (107 other events, 520.0 us)
Sparse Core Ops, SparseCore 0:
  11.0 61.6 all-gather.9
  75.5 59.0 all-gather.11
  137.6 57.4 all-gather.13
  364.8 17.3 all-reduce.15
  385.1 61.8 all-gather.17
  450.0 59.3 all-gather.15
  512.4 59.3 all-gather.19
  588.9 19.8 all-reduce.17
  703.2 15.7 reduce-scatter.14
  829.6 31.6 all-reduce.19
  863.6 77.7 reduce-scatter.36
  944.2 72.9 reduce-scatter.24
  1019.9 74.1 reduce-scatter.28
  1096.9 74.1 reduce-scatter.22
  1173.8 91.9 reduce-scatter.34
  1271.2 129.0 reduce-scatter.26
  1403.0 94.9 reduce-scatter.30
  1500.7 93.7 reduce-scatter.32
  1600.0 129.2 reduce-scatter.16
  1734.7 129.9 reduce-scatter.18
  1867.6 77.0 reduce-scatter.20
where the time goes:
time: 1960 us; the launch traced here: 1950 us
  waiting for transfers between devices  1170 us (60%)
  blocking collectives  310 us (16%)
  matrix products  302 us (15%)
  other arithmetic  85.2 us (4%)
  local copies, waits for them, and re-layouts  53.8 us (3%)
    reduce_scatter x1, waiting for transfers between devices, shards(): lax.psum_scatter(grad_input_w, ('shard', 'ctx'), scatter_dimension=0, til...  135 us
    reduce_scatter x1, waiting for transfers between devices, shards(): lax.psum_scatter(grad_gate_w, ('shard', 'ctx'), scatter_dimension=0, tile...  135 us
    reduce_scatter x1, waiting for transfers between devices, shards(): lax.psum_scatter(grad_mixout, ('shard', 'ctx'), scatter_dimension=1, tile...  135 us
    reduce_scatter x1, waiting for transfers between devices, shards(): lax.psum_scatter(grad_ffngate, ('shard', 'ctx'), scatter_dimension=0, til...  97.7 us
    reduce_scatter x1, waiting for transfers between devices, shards(): lax.psum_scatter(grad_ffnup, ('shard', 'ctx'), scatter_dimension=0, tiled...  96.5 us
    dot_general x3, matrix products, span_outputs(): jnp.einsum('stuh,suha->stha', mixing, inner_act, precision=highest)  95.6 us
    reduce_scatter x1, waiting for transfers between devices, shards(): lax.psum_scatter(grad_ffndown, ('shard', 'ctx'), scatter_dimension=1, til...  94.8 us
    reduce_scatter x1, waiting for transfers between devices, shards(): lax.psum_scatter(grad_state_w, ('shard', 'ctx'), scatter_dimension=0, til...  79.9 us
  transfers between devices with their start and end apart: 24, of which 16 were waited for; matrix products, arithmetic and copies ran while one was open for 16% of the time, Pallas kernels for 0%

commit v1 on v0

--- a/solution.py
+++ b/solution.py
@@ -4,7 +4,7 @@
 from jax.sharding import PartitionSpec as P
 
 epsilon = 1e-05
-highest = lax.Precision.HIGHEST
+highest = lax.Precision.HIGH
 
 
 def shifted(block, axis, distance):
@@ -199,32 +199,23 @@
     return (grad_query, jnp.concatenate([grad_keys, grad_vals], axis=1))
 
 
-def fetch_weights(
-    ssm_gate,
-    ssm_input,
-    ssm_state,
-    ssm_step,
-    attn_query,
-    attn_keyval,
-    ssm_out,
-    attn_out,
-    ffn_gate,
-    ffn_up,
-    ffn_down,
-):
-    return (
-        lax.all_gather(ssm_gate, ("shard", "ctx"), axis=0, tiled=True),
-        lax.all_gather(ssm_input, ("shard", "ctx"), axis=0, tiled=True),
-        lax.all_gather(ssm_state, ("shard", "ctx"), axis=0, tiled=True),
-        lax.all_gather(ssm_step, ("shard", "ctx"), axis=0, tiled=True),
-        lax.all_gather(attn_query, ("shard", "ctx"), axis=0, tiled=True),
-        lax.all_gather(attn_keyval, ("shard", "ctx"), axis=0, tiled=True),
-        lax.all_gather(ssm_out, ("shard", "ctx"), axis=1, tiled=True),
-        lax.all_gather(attn_out, ("shard", "ctx"), axis=1, tiled=True),
-        lax.all_gather(ffn_gate, ("shard", "ctx"), axis=0, tiled=True),
-        lax.all_gather(ffn_up, ("shard", "ctx"), axis=0, tiled=True),
-        lax.all_gather(ffn_down, ("shard", "ctx"), axis=1, tiled=True),
-    )
+def gather_rows(parts):
+    return lax.all_gather(jnp.concatenate(parts, axis=1), ("shard", "ctx"), axis=0, tiled=True)
+
+
+def scatter_rows(parts):
+    whole = jnp.concatenate([part.astype(jnp.bfloat16) for part in parts], axis=1)
+    return lax.psum_scatter(whole, ("shard", "ctx"), scatter_dimension=0, tiled=True).astype(
+        jnp.float32
+    )
+
+
+def split_columns(whole, widths):
+    parts, start = ([], 0)
+    for width in widths:
+        parts.append(whole[:, start : start + width])
+        start += width
+    return parts
 
 
 def fetch_keys(keyval_low):
@@ -264,44 +255,39 @@
     query_width = attn_query.shape[1]
     query_heads = query_width // head_dim
     offset = lax.axis_index("ctx") * span_len
-    gathered = fetch_weights(
-        ssm_gate,
-        ssm_input,
-        ssm_state,
-        ssm_step,
-        attn_query,
-        attn_keyval,
-        ssm_out,
-        attn_out,
-        ffn_gate,
-        ffn_up,
-        ffn_down,
-    )
-    (
-        full_gate,
-        full_input,
-        full_state,
-        full_step,
-        full_query,
-        full_keyval,
-        full_mixout,
-        full_attnout,
-        full_ffngate,
-        full_ffnup,
-        full_ffndown,
-    ) = gathered
-    keyval_flat = full_keyval.reshape(model_width, 2 * head_dim)
+    keyval_width = 2 * head_dim
+    ffn_width = ffn_gate.shape[1]
+    step_pad = -local_heads % 128
+    mixer_in_weights = gather_rows(
+        [
+            ssm_gate,
+            ssm_input,
+            ssm_state,
+            attn_query,
+            attn_keyval.reshape(-1, keyval_width),
+            jnp.pad(ssm_step, ((0, 0), (0, step_pad))),
+        ]
+    )
+    mixer_in_widths = (
+        inner_width,
+        inner_width,
+        2 * state_width,
+        query_width,
+        keyval_width,
+        local_heads + step_pad,
+    )
+    mixer_out_weights = gather_rows([ssm_out.T, attn_out.T])
+    ffn_in_weights = gather_rows([ffn_gate, ffn_up])
+    ffn_out_weights = gather_rows([ffn_down.T])
     inputs = tokens.reshape(row_count, model_width).astype(jnp.float32)
     inv_rms = lax.rsqrt(jnp.mean(inputs * inputs, axis=1, keepdims=True) + epsilon)
     normed = (inputs * inv_rms * mix_gain).astype(jnp.bfloat16)
-    gate_lin = matmul(normed, full_gate)
-    mixer_low = jnp.concatenate(
-        [matmul(normed, full_input), matmul(normed, full_state)], axis=1
-    ).astype(jnp.bfloat16)
+    gate_lin, input_lin, state_lin, queries, keyval, step_wide = split_columns(
+        matmul(normed, mixer_in_weights), mixer_in_widths
+    )
+    mixer_low = jnp.concatenate([input_lin, state_lin], axis=1).astype(jnp.bfloat16)
     mixer_low = mixer_low.reshape(seq_count, span_len, inner_width + 2 * state_width)
-    step_lin = matmul(normed, full_step)
-    queries = matmul(normed, full_query)
-    keyval = matmul(normed, keyval_flat)
+    step_lin = step_wide[:, :local_heads]
     rim_rows = shifted(mixer_low[:, span_len - tap_count + 1 :], "ctx", 1)
     padded = jnp.concatenate([rim_rows, mixer_low], axis=1).astype(jnp.float32)
     conv_taps = jnp.concatenate([conv_input, conv_state], axis=1)
@@ -347,6 +333,7 @@
         local_mixer, inner_act, input_mat, output_mat, step_size, decay_rate
     )
     ssm_flat = mixer_values[0].reshape(row_count, inner_width)
+    ssm_flat, ffn_in_weights = lax.optimization_barrier((ssm_flat, ffn_in_weights))
     gated = (ssm_flat * jax.nn.silu(gate_lin)).astype(jnp.bfloat16)
     cos_table, sin_table = rotary_tables(offset + jnp.arange(span_len), head_dim)
     rotated_q = rotate(
@@ -366,60 +353,33 @@
 
     attended, log_total = lax.map(forward_one, (rotated_q, all_keys, segments, seg_part))
     attended_low = attended.reshape(row_count, query_width).astype(jnp.bfloat16)
+    mixed_low = jnp.concatenate([gated, attended_low], axis=1)
     mixer_sum = lax.psum(
-        (matmul(gated, full_mixout) + matmul(attended_low, full_attnout)).astype(jnp.bfloat16), "tp"
+        back_product(mixed_low, mixer_out_weights).astype(jnp.bfloat16), "tp"
     ).astype(jnp.float32)
+    mixer_sum, ffn_out_weights = lax.optimization_barrier((mixer_sum, ffn_out_weights))
     hidden = inputs + mixer_sum
     inv_rms_ffn = lax.rsqrt(jnp.mean(hidden * hidden, axis=1, keepdims=True) + epsilon)
     normed_ffn = (hidden * inv_rms_ffn * ffn_gain).astype(jnp.bfloat16)
-    gate_ffn = matmul(normed_ffn, full_ffngate)
-    up_ffn = matmul(normed_ffn, full_ffnup)
+    gate_ffn, up_ffn = split_columns(matmul(normed_ffn, ffn_in_weights), (ffn_width, ffn_width))
     act_ffn = (jax.nn.silu(gate_ffn) * up_ffn).astype(jnp.bfloat16)
-    ffn_result = lax.psum(matmul(act_ffn, full_ffndown).astype(jnp.bfloat16), "tp").astype(
+    ffn_result = lax.psum(back_product(act_ffn, ffn_out_weights).astype(jnp.bfloat16), "tp").astype(
         jnp.float32
     )
     layer_out = (hidden + ffn_result).astype(jnp.bfloat16).reshape(seq_count, span_len, model_width)
-    weights_back = fetch_weights(
-        ssm_gate,
-        ssm_input,
-        ssm_state,
-        ssm_step,
-        attn_query,
-        attn_keyval,
-        ssm_out,
-        attn_out,
-        ffn_gate,
-        ffn_up,
-        ffn_down,
-    )
-    (
-        back_gate,
-        back_input,
-        back_state,
-        back_step,
-        back_query,
-        back_keyval,
-        back_mixout,
-        back_attnout,
-        back_ffngate,
-        back_ffnup,
-        back_ffndown,
-    ) = weights_back
-    back_keyval_flat = back_keyval.reshape(model_width, 2 * head_dim)
     grad_out = cotangent.reshape(row_count, model_width)
-    grad_act = back_product(grad_out, back_ffndown)
-    grad_ffndown = weight_grad(act_ffn, grad_out)
+    grad_act = matmul(grad_out, ffn_out_weights)
+    grad_ffndown = weight_grad(grad_out, act_ffn)
     sig_gate = jax.nn.sigmoid(gate_ffn)
     grad_up = (grad_act * gate_ffn * sig_gate).astype(jnp.bfloat16)
     grad_gate = (grad_act * up_ffn * sig_gate * (1.0 + gate_ffn * (1.0 - sig_gate))).astype(
         jnp.bfloat16
     )
-    grad_ffngate = weight_grad(normed_ffn, grad_gate)
-    grad_ffnup = weight_grad(normed_ffn, grad_up)
+    grad_ffn_low = jnp.concatenate([grad_gate, grad_up], axis=1)
+    grad_ffnin = weight_grad(normed_ffn, grad_ffn_low)
+    summed_ffn = scatter_rows([grad_ffnin, grad_ffndown])
     grad_normed_ffn = lax.psum(
-        (back_product(grad_gate, back_ffngate) + back_product(grad_up, back_ffnup)).astype(
-            jnp.bfloat16
-        ),
+        back_product(grad_ffn_low, ffn_in_weights).astype(jnp.bfloat16),
         "tp",
     ).astype(jnp.float32)
     grad_ffn_gain = jnp.sum(grad_normed_ffn * hidden * inv_rms_ffn, axis=0)
@@ -430,13 +390,12 @@
         - hidden * inv_rms_ffn**3 * jnp.mean(scaled_ffn * hidden, axis=1, keepdims=True)
     )
     grad_hidden_low = grad_hidden.astype(jnp.bfloat16)
-    grad_mixout = weight_grad(gated, grad_hidden_low)
-    grad_attnout = weight_grad(attended_low, grad_hidden_low)
-    grad_gated = back_product(grad_hidden_low, back_mixout)
-    grad_attended = (
-        back_product(grad_hidden_low, back_attnout)
-        .astype(jnp.bfloat16)
-        .reshape(seq_count, span_len, query_heads, head_dim)
+    summed_mixout = scatter_rows([weight_grad(grad_hidden_low, mixed_low)])
+    grad_gated, grad_attended = split_columns(
+        matmul(grad_hidden_low, mixer_out_weights), (inner_width, query_width)
+    )
+    grad_attended = grad_attended.astype(jnp.bfloat16).reshape(
+        seq_count, span_len, query_heads, head_dim
     )
     sig_zeta = jax.nn.sigmoid(gate_lin)
     grad_ssm = (grad_gated * gate_lin * sig_zeta).reshape(
@@ -460,6 +419,9 @@
     grad_inner, grad_input_mat, grad_output_mat, grad_step, grad_decay_rate = mixer_pull(
         (grad_ssm, later_grad, grad_link)
     )
+    grad_inner, grad_input_mat, grad_output_mat, grad_step, summed_ffn = lax.optimization_barrier(
+        (grad_inner, grad_input_mat, grad_output_mat, grad_step, summed_ffn)
+    )
     grad_step_lin = grad_step.reshape(row_count, local_heads) * jax.nn.sigmoid(step_lin + step_bias)
     grad_step_bias = jnp.sum(grad_step_lin, axis=0)
     grad_step_low = grad_step_lin.astype(jnp.bfloat16)
@@ -506,12 +468,19 @@
         axis=-1,
     )
     grad_keyval_low = grad_keyval_low.reshape(row_count, 2 * head_dim).astype(jnp.bfloat16)
+    gate_w, input_w, state_w, query_w, keyval_w, step_w = split_columns(
+        mixer_in_weights, mixer_in_widths
+    )
+    grad_step_wide = jnp.pad(grad_step_low, ((0, 0), (0, step_pad)))
+    grad_queries, grad_keyval_low, summed_mixout = lax.optimization_barrier(
+        (grad_queries, grad_keyval_low, summed_mixout)
+    )
     grad_norm_part = (
-        back_product(grad_zeta, back_gate)
-        + back_product(grad_mixer_inner, back_input)
-        + back_product(grad_step_low, back_step)
-        + back_product(grad_queries, back_query)
-        + back_product(grad_keyval_low, back_keyval_flat)
+        back_product(grad_zeta, gate_w)
+        + back_product(grad_mixer_inner, input_w)
+        + back_product(grad_step_wide, step_w)
+        + back_product(grad_queries, query_w)
+        + back_product(grad_keyval_low, keyval_w)
     )
     grad_norm_sum, grad_conv_state = (
         lax.psum(grad_norm_part.astype(jnp.bfloat16), "tp").astype(jnp.float32),
@@ -526,7 +495,7 @@
         .astype(jnp.bfloat16)
         .reshape(row_count, 2 * state_width)
     )
-    grad_normed = grad_norm_sum + back_product(grad_mixer_state, back_state)
+    grad_normed = grad_norm_sum + back_product(grad_mixer_state, state_w)
     grad_mix_gain = jnp.sum(grad_normed * inputs * inv_rms, axis=0)
     scaled_mix = grad_normed * mix_gain
     grad_tokens = (
@@ -534,52 +503,53 @@
         + inv_rms * scaled_mix
         - inputs * inv_rms**3 * jnp.mean(scaled_mix * inputs, axis=1, keepdims=True)
     )
-    grad_gate_w = weight_grad(normed, grad_zeta)
-    grad_input_w = weight_grad(normed, grad_mixer_inner)
-    grad_state_w = weight_grad(normed, grad_mixer_state)
-    grad_step_w = weight_grad(normed, grad_step_low)
-    grad_query_w = weight_grad(normed, grad_queries)
-    grad_keyval_w = weight_grad(normed, grad_keyval_low).reshape(model_width, 1, 2 * head_dim)
-    summed = (
-        lax.psum_scatter(grad_gate_w, ("shard", "ctx"), scatter_dimension=0, tiled=True),
-        lax.psum_scatter(grad_input_w, ("shard", "ctx"), scatter_dimension=0, tiled=True),
-        lax.psum_scatter(grad_state_w, ("shard", "ctx"), scatter_dimension=0, tiled=True),
-        lax.psum_scatter(grad_step_w, ("shard", "ctx"), scatter_dimension=0, tiled=True),
-        lax.psum_scatter(grad_query_w, ("shard", "ctx"), scatter_dimension=0, tiled=True),
-        lax.psum_scatter(grad_keyval_w, ("shard", "ctx"), scatter_dimension=0, tiled=True),
-        lax.psum_scatter(grad_mixout, ("shard", "ctx"), scatter_dimension=1, tiled=True),
-        lax.psum_scatter(grad_attnout, ("shard", "ctx"), scatter_dimension=1, tiled=True),
-        lax.psum_scatter(grad_ffngate, ("shard", "ctx"), scatter_dimension=0, tiled=True),
-        lax.psum_scatter(grad_ffnup, ("shard", "ctx"), scatter_dimension=0, tiled=True),
-        lax.psum_scatter(grad_ffndown, ("shard", "ctx"), scatter_dimension=1, tiled=True),
-    )
-    small_sums = lax.psum(
-        (
-            grad_taps_inner,
-            grad_taps_state,
-            grad_step_bias,
-            grad_decay_rate,
-            grad_mix_gain,
-            grad_ffn_gain,
-        ),
-        ("shard", "ctx"),
-    )
+    grad_mixer_low = jnp.concatenate(
+        [
+            grad_zeta,
+            grad_mixer_inner,
+            grad_mixer_state,
+            grad_queries,
+            grad_keyval_low,
+            grad_step_wide,
+        ],
+        axis=1,
+    )
+    summed_in = split_columns(
+        scatter_rows([weight_grad(normed, grad_mixer_low)]), mixer_in_widths
+    )
+    summed_out = split_columns(summed_mixout, (inner_width, query_width))
+    summed_gate, summed_up, summed_down = split_columns(summed_ffn, (ffn_width,) * 3)
+    small_parts = (
+        grad_taps_inner,
+        grad_taps_state,
+        grad_step_bias,
+        grad_decay_rate,
+        grad_mix_gain,
+        grad_ffn_gain,
+    )
+    small_flat = jnp.concatenate([part.reshape(-1) for part in small_parts])
+    small_flat = jnp.pad(small_flat, (0, -small_flat.shape[0] % 1024)).reshape(-1, 128)
+    small_total = jnp.sum(lax.all_gather(small_flat, ("shard", "ctx")), axis=0).reshape(-1)
+    small_sums, start = ([], 0)
+    for part in small_parts:
+        small_sums.append(small_total[start : start + part.size].reshape(part.shape))
+        start += part.size
     return (
         layer_out,
         grad_tokens.reshape(seq_count, span_len, model_width),
         small_sums[4],
         small_sums[5],
-        summed[0],
-        summed[1],
-        summed[2],
-        summed[3],
-        summed[4],
-        summed[5],
-        summed[6],
-        summed[7],
-        summed[8],
-        summed[9],
-        summed[10],
+        summed_in[0],
+        summed_in[1],
+        summed_in[2],
+        summed_in[5][:, :local_heads],
+        summed_in[3],
+        summed_in[4].reshape(-1, 1, keyval_width),
+        summed_out[0].T,
+        summed_out[1].T,
+        summed_gate,
+        summed_up,
+        summed_down.T,
         small_sums[0],
         small_sums[1],
         small_sums[2],

time: 1960 us -> 898 us (0.46)
  waiting for transfers between devices: 1170 us -> 341 us
  blocking collectives: 310 us -> 95.6 us
  matrix products: 302 us -> 201 us
  local copies, waits for them, and re-layouts: 53.8 us -> 103 us
  other arithmetic: 85.2 us -> 125 us
    reduce_scatter x10 -> x3, waiting for transfers between devices: 917 us -> 133 us  [scatter_rows(): lax.psum_scatter(whole, ('shard', 'ctx'), scatter_dimension=0, tiled=True)]
    all_gather x5 -> x1, blocking collectives: 206 us -> 44.4 us  [shards(): lax.all_gather(small_flat, ('shard', 'ctx'))]
    psum x1 -> x0, blocking collectives: 72.1 us -> none  [shards(): lax.psum((grad_taps_inner, grad_taps_state, grad_step_bias, grad_decay_ra...]
    unnamed x22 -> x11, waiting for transfers between devices: 55.8 us -> 0.7 us
    psum x3, waiting for transfers between devices: 27.7 us -> 65.9 us  [the longest x1 26.5 us: shards(): lax.psum(grad_conv[..., inner_width:].astype(jnp.bfloat16), 'tp')]
    all_gather x6 -> x4, waiting for transfers between devices: 171 us -> 136 us  [gather_rows(): lax.all_gather(jnp.concatenate(parts, axis=1), ('shard', 'ctx'), axis=0,...]
    dot_general x3, matrix products: 95.6 us -> 64 us  [span_outputs(): jnp.einsum('stuh,suha->stha', mixing, inner_act, precision=highest)]
    dot_general x10 -> x4, matrix products: 45.8 us -> 23.2 us  [weight_grad(): lax.dot_general(left_side, right_side, (((0,), (0,)), ((), ())), preferre...]
  transfers between devices with their start and end apart: 24 -> 14, of which waited for: 16 -> 10; matrix products, arithmetic and copies ran while one was open for 16% -> 34% of each run, Pallas kernels for 0% -> 0%
where the time goes in v1:
time: 898 us; the launch traced here: 890 us
  waiting for transfers between devices  341 us (38%)
  matrix products  201 us (22%)
  other arithmetic  125 us (14%)
  local copies, waits for them, and re-layouts  103 us (11%)
  blocking collectives  95.6 us (11%)
  between operations  16 us (2%)
    all_gather x4, waiting for transfers between devices, gather_rows(): lax.all_gather(jnp.concatenate(parts, axis=1), ('shard', 'ctx'), axis=0,...  136 us
    reduce_scatter x3, waiting for transfers between devices, scatter_rows(): lax.psum_scatter(whole, ('shard', 'ctx'), scatter_dimension=0, tiled=True)  133 us
    dot_general x3, matrix products, span_outputs(): jnp.einsum('stuh,suha->stha', mixing, inner_act, precision=highest)  64 us
    all_gather x1, blocking collectives, shards(): lax.all_gather(small_flat, ('shard', 'ctx'))  44.4 us
    dot_general x9, matrix products, back_product(): lax.dot_general(left_side, right_side, (((1,), (1,)), ((), ())), preferre...  39.6 us
    all_gather x3, blocking collectives, entering(): lax.all_gather(part.astype(kind), axis)  39.3 us
    unnamed x247, local copies, waits for them, and re-layouts  30.3 us
    psum x1, waiting for transfers between devices, shards(): lax.psum(grad_conv[..., inner_width:].astype(jnp.bfloat16), 'tp')  26.5 us
  transfers between devices with their start and end apart: 14, of which 10 were waited for; matrix products, arithmetic and copies ran while one was open for 34% of the time, Pallas kernels for 0%

profile of v1, /device:TPU:0, one launch (start us, length us, event | category | flops | bytes accessed | tf_op | source)
XLA Modules:
  0.0 890.4 jit_solution(15502106315486527617)
XLA Ops:
  26.0 70.4 %all-gather.7.cloned.1.call-done = bf16[1024,2304]{1,0:T(8,128)(2,1)} async-done(((bf16[64,2304]{1,0:T(8,128)(2,1)}), bf16[1024,2304]{1,0:T(8,128)(2,1)}) %all-gather.7.cloned.1.call-update) | async-done | bytes 4718608 | tf_op jit(solution)/shard_map/all_gather | solution.py:203
  96.4 8.0 fusion.187
  116.3 4.0 collective-permute-start
  121.7 11.8 %all_gather.42 = bf16[2,1024,128]{1,2,0:T(8,128)(2,1)S(1)} all-gather(bf16[2,512,128]{1,2,0:T(8,128)(2,1)S(1)} %pad_maximum_fusion.14), channel_id=1, replica_groups=mesh['shard'=8,'ctx'=2,'tp'=2] {'ctx'}, dimensions={1}, use_global_device_ids=true | all-gather | bytes 786432 | tf_op jit(solution)/shard_map/all_gather | solution.py:222
  141.8 14.2 %while.54 = (s32[]{:T(128)}, bf16[2,512,4,64]{1,3,2,0:T(8,128)(2,1)}, f32[2,4,512,1]{2,1,3,0:T(4,128)S(1)}, bf16[2,1024,128]{1,2,0:T(8,128)(2,1)S(1)}, s32[]{:T(...) while((s32[]{:T(128)}, ...), condition=%wide.region_8.9_spmd, body=%wide.region_5.8_spmd.sunk | while | flops 561510912 | bytes 33118384 | solution.py:354
  156.3 4.2 all_gather.38
  167.0 3.8 fusion.92
  180.1 9.7 %all-gather = bf16[4,12,64,128]{3,2,1,0:T(8,128)(2,1)} all-gather(bf16[2,12,64,128]{3,2,1,0:T(8,128)(2,1)S(1)} %fusion.123), channel_id=2, replica_groups=mesh['shard'=8,'ctx'=2,'tp'=2] {'ctx'}, dimensions={0}, use_global_device_ids=true | all-gather | bytes 1179648 | tf_op jit(solution)/shard_map/all_gather | solution.py:19
  193.3 4.4 while.56
  202.2 17.3 %bitcast_add_fusion.2 = f32[2,512,12,64]{1,3,2,0:T(8,128)S(1)} fusion(f32[2,512,12,64]{1,3,2,0:T(8,128)S(1)} %fusion.141, f32[2,512,12,64]{1,3,2,0:T(8,128)S(1)} %bitcast.395, f32[2,512,12]{1,2,0:T(8,128)S(1)} %get-tuple-element.717, f32[2,512,12]{1,2,0:T(8,128)S(1)} %bitcast.424, f32[2,512,512]{2,1,0:T(8,128)S(1)} %copy-done.36, ...), kind=kOutput, calls=%fused_computation.161 | convolution fusion | flops 2448949248 | bytes 12206080 | tf_op jit(solution)/shard_map/jvp(stuh,suha->stha)/dot_general | solution.py:113
  226.7 5.1 multiply_convert_fusion.3
  231.7 5.2 all-gather.11.cloned.1.call-done
  236.9 5.9 convolution_convert_fusion.4
  243.5 19.4 %all-reduce.18.cloned.1.call-done = bf16[1024,1024]{1,0:T(8,128)(2,1)} async-done(((bf16[1024,1024]{1,0:T(8,128)(2,1)}), bf16[1024,1024]{1,0:T(8,128)(2,1)}) %all-reduce.18.cloned.1.call-update) | async-done | bytes 2097168 | tf_op jit(solution)/shard_map/psum | solution.py:357
  262.9 4.0 convert_element_type.256
  266.9 60.8 %all-gather.13.cloned.1.call-done = bf16[1024,1024]{1,0:T(8,128)(2,1)} async-done(((bf16[64,1024]{1,0:T(8,128)(2,1)}), bf16[1024,1024]{1,0:T(8,128)(2,1)}) %all-gather.13.cloned.1.call-update) | async-done | bytes 2097168 | tf_op jit(solution)/shard_map/all_gather | solution.py:203
  331.2 4.6 fusion.176
  335.8 5.6 fusion.81
  343.4 5.8 fusion.107
  349.3 19.9 %all-reduce.20.cloned.1.call-done = bf16[1024,1024]{1,0:T(8,128)(2,1)} async-done(((bf16[1024,1024]{1,0:T(8,128)(2,1)}), bf16[1024,1024]{1,0:T(8,128)(2,1)}) %all-reduce.20.cloned.1.call-update) | async-done | bytes 2097168 | tf_op jit(solution)/shard_map/psum | solution.py:381
  369.2 4.9 fusion.74
  380.6 35.0 %while.55 = (s32[]{:T(128)}, f32[2,512,4,64]{1,0,3,2:T(2,128)S(1)}, bf16[2,1024,128]{1,2,0:T(8,128)(2,1)}, bf16[2,1024,128]{1,2,0:T(8,128)(2,1)S(1)}, s32[]{:T(1...) while((s32[]{:T(128)}, f32[2,512,4,64]{1,0,3,2:T(2,128)S(1)}, ...), condition=%wide.region_29.30_spmd, body=%wide.region_27.29_spmd.sunk | while | flops 1375992320 | bytes 74660048 | solution.py:452
  393.3 4.9 dynamic_update_slice.25
  410.7 4.9 dynamic_update_slice.25
  415.7 6.9 convolution_convert_fusion.2
  423.6 4.1 convert_bitcast_fusion
  427.7 5.4 convolution_convert_fusion.1
  437.9 5.5 convolution_convert_fusion.3
  447.8 5.5 multiply_multiply_fusion
  456.9 4.3 reshape.615
  464.4 25.4 %all-gather.1 = bf16[4,12,64,128]{3,2,1,0:T(8,128)(2,1)} all-gather(bf16[2,12,64,128]{3,2,1,0:T(8,128)(2,1)S(1)} %fusion.122), channel_id=3, replica_groups=mesh['shard'=8,'ctx'=2,'tp'=2] {'ctx'}, dimensions={0}, use_global_device_ids=true | all-gather | bytes 1179648 | tf_op jit(solution)/shard_map/all_gather | solution.py:19
  489.8 4.6 while.57
  496.1 4.5 multiply_reduce_fusion.3
  501.2 3.9 multiply_reduce_fusion.2
  505.6 29.8 %fusion.55 = (f32[2,512,12]{1,2,0:T(8,128)S(1)}, f32[2,512,12]{1,2,0:T(8,128)S(1)}, f32[2,512,12]{1,2,0:T(8,128)}, f32[2,512,512]{2,1,0:T(8,128)}) fusion(f32[2,512,12]{1,2,0:T(8,128)S(1)} %copy-done.70, f32[2,512,12]{1,2,0:T(8,128)S(1)} %bitcast.426, f32[2,512,512]{2,1,0:T(8,128)S(1)} %copy-done.37, pred[2,512,512]{2,1,0:T(8,128)(4,1)S(1)} %copy-done.62, ...), kind=kOutput, calls=%fused_computation.85 | convolution fusion | flops 2509729792 | bytes 11255808 | tf_op jit(solution)/shard_map/transpose(jvp(stuh,suha->stha))/dot_general | solution.py:113
  539.1 11.4 %reduce-window.16 = f32[2,12,4,128]{3,1,2,0:T(8,128)} reduce-window(f32[2,12,4,128]{3,1,2,0:T(8,128)} %copy.271, f32[]{:T(128)} %constant.159.clone.1), window={size=1x1x1x128 pad=0_0x0_0x0_0x0_127}, to_apply=%region_24.25 | reduce-window | flops 1560576 | bytes 98308 | tf_op jit(solution)/shard_map/reduce-window.2
  571.9 4.4 constant_dynamic-update-slice_fusion.13
  576.3 5.5 fusion.116
  581.8 16.8 %bitcast_add_fusion.1 = f32[2,512,12,64]{1,3,2,0:T(8,128)} fusion(f32[2,512,12,64]{1,3,2,0:T(8,128)S(1)} %copy-done.35, f32[2,512,12]{1,2,0:T(8,128)S(1)} %copy-done.71, f32[2,512,12]{1,2,0:T(8,128)S(1)} %bitcast.427, f32[2,512,512]{2,1,0:T(8,128)S(1)} %copy-done.38, pred[2,512,512]{2,1,0:T(8,128)(4,1)S(1)} %copy-done.63, ...), kind=kOutput, calls=%fused_computation.160 | convolution fusion | flops 2448949248 | bytes 12206080 | tf_op jit(solution)/shard_map/transpose(jvp(stuh,suha->stha))/dot_general | solution.py:113
  602.5 3.9 fusion.138
  606.4 58.6 %reduce-scatter.5.cloned.1.call-done = bf16[64,3072]{1,0:T(8,128)(2,1)} async-done(((bf16[1024,3072]{1,0:T(8,128)(2,1)}), bf16[64,3072]{1,0:T(8,128)(2,1)}) %reduce-scatter.5.cloned.1.call-update) | async-done | bytes 393232 | tf_op jit(solution)/shard_map/reduce_scatter | solution.py:208
  694.6 26.5 %all-reduce.22.cloned.1.call-done = (bf16[2,512,256]{2,1,0:T(8,128)(2,1)}, bf16[1024,1024]{1,0:T(8,128)(2,1)}, bf16[1024,1024]{1,0:T(8,128)(2,1)}) async-done(((bf16[2,512,256]{2,1,0:T(8,128)(2,1)}, bf16[1024,1024]{1,0:T(8,128)(2,1)}, bf16[1024,1024]{1,0:T(8,128)(2,1)}), (bf16[2,512,256]{2,1,0:T(8,128)(2,1)}, bf16[1024,1024]{1,0:T(8,128)(2,1)}, bf16[1024,1024]{1,0:T(8,128)(2,1)})) %all-reduce.22.cloned.1.call-update) | async-done | bytes 4718608 | tf_op jit(solution)/shard_map/psum | solution.py:487
  730.8 6.8 convolution_convert_fusion
  741.0 5.1 add_convert_fusion.1
  746.1 4.6 fusion.91
  750.8 44.4 %all_gather.47 = f32[16,56,128]{2,1,0:T(8,128)S(1)} all-gather(f32[1,56,128]{2,1,0:T(8,128)S(1)} %pad_bitcast_fusion), channel_id=1, replica_groups=mesh['shard'=8,'ctx'=2,'tp'=2] {'shard','ctx'}, dimensions={0}, use_global_device_ids=true | all-gather | bytes 487424 | tf_op jit(solution)/shard_map/all_gather | solution.py:532
  797.7 5.4 fusion.88
  803.1 74.4 %reduce-scatter.11.cloned.1.call-done = bf16[64,2304]{1,0:T(8,128)(2,1)} async-done(((bf16[1024,2304]{1,0:T(8,128)(2,1)}), bf16[64,2304]{1,0:T(8,128)(2,1)}) %reduce-scatter.11.cloned.1.call-update) | async-done | bytes 294928 | tf_op jit(solution)/shard_map/reduce_scatter | solution.py:208
  (500 shorter events, 230.4 us)
Async XLA Ops:
  7.2 16.6 %copy-start.11 = (bf16[2,512,1024]{2,1,0:T(8,128)(2,1)S(1)}, bf16[2,512,1024]{2,1,0:T(8,128)(2,1)}, u32[]{:S(2)}) copy-start(bf16[2,512,1024]{2,1,0:T(8,128)(2,1)} %param.28) | copy-start | bytes 6291460
  7.2 14.6 %copy-start.76 = (f32[4,768]{1,0:T(4,128)S(1)}, f32[4,768]{1,0:T(4,128)}, u32[]{:S(2)}) copy-start(f32[4,768]{1,0:T(4,128)} %param.44) | copy-start | bytes 36868
  7.2 14.6 %copy-start.88 = (f32[4,256]{1,0:T(4,128)S(1)}, f32[4,256]{1,0:T(4,128)}, u32[]{:S(2)}) copy-start(f32[4,256]{1,0:T(4,128)} %param.45) | copy-start | bytes 12292
  7.2 16.6 %copy-start.90 = (f32[1024]{0:T(1024)S(1)}, f32[1024]{0:T(1024)}, u32[]{:S(2)}) copy-start(f32[1024]{0:T(1024)} %param.31) | copy-start | bytes 12292
  7.2 89.1 %all-gather.7.cloned.1.call-start = ((), (), s32[]{:S(2)}) async-start(), calls=%async_computation.4 | async-start | bytes 5013504 | tf_op jit(solution)/shard_map/all_gather | solution.py:203
  13.0 211.3 %all-gather.9.cloned.1.call-start = ((), (), s32[]{:S(2)}) async-start(), calls=%async_computation.5 | async-start | bytes 4456448 | tf_op jit(solution)/shard_map/all_gather | solution.py:203
  14.8 222.1 %all-gather.11.cloned.1.call-start = ((), (), s32[]{:S(2)}) async-start(), calls=%async_computation.6 | async-start | bytes 2228224 | tf_op jit(solution)/shard_map/all_gather | solution.py:203
  16.4 246.5 %all-reduce.18.cloned.1.call-start = ((), (), s32[]{:S(2)}) async-start(), calls=%async_computation.7 | async-start | bytes 4194304 | tf_op jit(solution)/shard_map/psum | solution.py:357
  19.7 136.4 %copy-start.82 = (pred[2,512]{1,0:T(4,128)(4,1)}, pred[2,512]{1,0:T(4,128)(4,1)S(1)}, u32[]{:S(2)}) copy-start(pred[2,512]{1,0:T(4,128)(4,1)S(1)} %get-tuple-element.677) | copy-start | bytes 3076
  21.8 82.6 %copy-start.72 = (f32[1,4,2,128]{3,1,2,0:T(4,128)}, f32[1,4,2,128]{3,1,2,0:T(4,128)S(1)}, u32[]{:S(2)}) copy-start(f32[1,4,2,128]{3,1,2,0:T(4,128)S(1)} %copy.358) | copy-start | bytes 12292
  22.6 133.5 %copy-start.74 = (pred[2,512]{1,0:T(4,128)(4,1)}, pred[2,512]{1,0:T(4,128)(4,1)S(1)}, u32[]{:S(2)}) copy-start(pred[2,512]{1,0:T(4,128)(4,1)S(1)} %broadcast_compare_fusion.1) | copy-start | bytes 3076
  26.0 113.3 %copy-start.46 = (f32[512,32]{0,1:T(8,128)}, f32[512,32]{0,1:T(8,128)S(1)}, u32[]{:S(2)}) copy-start(f32[512,32]{0,1:T(8,128)S(1)} %get-tuple-element.732) | copy-start | bytes 196612
  26.0 113.3 %copy-start.48 = (f32[512,32]{0,1:T(8,128)}, f32[512,32]{0,1:T(8,128)S(1)}, u32[]{:S(2)}) copy-start(f32[512,32]{0,1:T(8,128)S(1)} %get-tuple-element.733) | copy-start | bytes 196612
  110.8 45.4 %copy-start.44 = (f32[2,512,12]{1,0,2:T(2,128)}, f32[2,512,12]{1,0,2:T(2,128)S(1)}, u32[]{:S(2)}) copy-start(f32[2,512,12]{1,0,2:T(2,128)S(1)} %reshape.607) | copy-start | bytes 147460
  114.9 85.6 %copy-start.42 = (f32[2,12,512]{2,1,0:T(8,128)}, f32[2,12,512]{2,1,0:T(8,128)S(1)}, u32[]{:S(2)}) copy-start(f32[2,12,512]{2,1,0:T(8,128)S(1)} %reshape.651) | copy-start | bytes 147460
  115.6 40.5 %copy-start.78 = (f32[2,12]{1,0:T(2,128)}, f32[2,12]{1,0:T(2,128)S(1)}, u32[]{:S(2)}) copy-start(f32[2,12]{1,0:T(2,128)S(1)} %get-tuple-element.600) | copy-start | bytes 292
  116.3 49.3 %collective-permute-start = (bf16[2,3,1024]{2,1,0:T(4,128)(2,1)}, bf16[2,3,1024]{2,1,0:T(4,128)(2,1)}, u32[]{:S(2)}, u32[]{:S(2)}) collective-permute-start(bf16[2,3,1024]{2,1,0:T(4,128)(2,1)} %slice.394), channel_id=1, source_target_pairs={{0,2},{1,3},{4,6},{5,7},{8,10},{9,11},{12,14},{13,15},{16,18},{17,... | collective-permute-start | bytes 36872 | tf_op jit(solution)/shard_map/ppermute | solution.py:13
  133.6 8.2 copy-start.67
  141.8 14.2 %copy-start.99 = (pred[2]{0:T(512)(128)(4,1)S(1)}, pred[2]{0:T(512)(128)(4,1)}, u32[]{:S(2)}) copy-start(pred[2]{0:T(512)(128)(4,1)} %compare_reduce_fusion) | copy-start | bytes 10
  141.8 14.2 %copy-start.101 = (bf16[2,12]{1,0:T(2,128)(2,1)S(1)}, bf16[2,12]{1,0:T(2,128)(2,1)}, u32[]{:S(2)}) copy-start(bf16[2,12]{1,0:T(2,128)(2,1)} %get-tuple-element.601) | copy-start | bytes 148
  156.0 10.9 %copy-start.20 = (bf16[2,512,4,64]{1,3,2,0:T(8,128)(2,1)}, bf16[2,512,4,64]{1,3,2,0:T(8,128)(2,1)S(1)}, u32[]{:S(2)}) copy-start(bf16[2,512,4,64]{1,3,2,0:T(8,128)(2,1)S(1)} %get-tuple-element.1049) | copy-start | bytes 1572868
  156.0 10.9 %copy-start.22 = (bf16[2,1024,128]{1,2,0:T(8,128)(2,1)}, bf16[2,1024,128]{1,2,0:T(8,128)(2,1)S(1)}, u32[]{:S(2)}) copy-start(bf16[2,1024,128]{1,2,0:T(8,128)(2,1)S(1)} %get-tuple-element.1050) | copy-start | bytes 1572868
  156.2 21.0 %copy-start.52 = (f32[2,512,12]{1,2,0:T(8,128)}, f32[2,512,12]{1,2,0:T(8,128)S(1)}, u32[]{:S(2)}) copy-start(f32[2,512,12]{1,2,0:T(8,128)S(1)} %get-tuple-element.716) | copy-start | bytes 147460
  156.2 44.3 %copy-start.54 = (f32[2,512,12]{1,2,0:T(8,128)}, f32[2,512,12]{1,2,0:T(8,128)S(1)}, u32[]{:S(2)}) copy-start(f32[2,512,12]{1,2,0:T(8,128)S(1)} %get-tuple-element.715) | copy-start | bytes 147460
  156.2 44.3 %copy-start.69 = (f32[2,512,12]{1,2,0:T(8,128)}, f32[2,512,12]{1,2,0:T(8,128)S(1)}, u32[]{:S(2)}) copy-start(f32[2,512,12]{1,2,0:T(8,128)S(1)} %get-tuple-element.717) | copy-start | bytes 147460
  177.2 23.4 %copy-start.4 = (f32[2,512,768]{1,2,0:T(8,128)}, f32[2,512,768]{1,2,0:T(8,128)S(1)}, u32[]{:S(2)}) copy-start(f32[2,512,768]{1,2,0:T(8,128)S(1)} %copy.238) | copy-start | bytes 9437188
  197.7 21.8 %copy-start.80 = (bf16[2,2,12]{2,1,0:T(2,128)(2,1)}, bf16[2,2,12]{2,1,0:T(2,128)(2,1)S(1)}, u32[]{:S(2)}) copy-start(bf16[2,2,12]{2,1,0:T(2,128)(2,1)S(1)} %get-tuple-element.1085) | copy-start | bytes 292
  226.7 16.2 %copy-start.15 = (f32[1024,768]{1,0:T(8,128)}, f32[1024,768]{1,0:T(8,128)S(1)}, u32[]{:S(2)}) copy-start(f32[1024,768]{1,0:T(8,128)S(1)} %copy.248) | copy-start | bytes 9437188
  242.8 84.9 %copy-start.12 = (bf16[2,512,1024]{2,1,0:T(8,128)(2,1)S(1)}, bf16[2,512,1024]{2,1,0:T(8,128)(2,1)}, u32[]{:S(2)}) copy-start(bf16[2,512,1024]{2,1,0:T(8,128)(2,1)} %param.28) | copy-start | bytes 6291460
  242.9 84.8 %all-gather.13.cloned.1.call-start = ((), (), s32[]{:S(2)}) async-start(), calls=%async_computation.8 | async-start | bytes 2228224 | tf_op jit(solution)/shard_map/all_gather | solution.py:203
  243.5 125.7 %all-reduce.20.cloned.1.call-start = ((), (), s32[]{:S(2)}) async-start(), calls=%async_computation.9 | async-start | bytes 4194304 | tf_op jit(solution)/shard_map/psum | solution.py:381
  266.9 63.8 %copy-start.84 = (f32[1024]{0:T(1024)S(1)}, f32[1024]{0:T(1024)}, u32[]{:S(2)}) copy-start(f32[1024]{0:T(1024)} %param.32) | copy-start | bytes 12292
  349.2 249.5 %reduce-scatter.7.cloned.1.call-start = ((), (), s32[]{:S(2)}) async-start(), calls=%async_computation.11 | async-start | bytes 786432 | tf_op jit(solution)/shard_map/reduce_scatter | solution.py:455
  415.7 185.2 %reduce-scatter.9.cloned.1.call-start = ((), (), s32[]{:S(2)}) async-start(), calls=%async_computation.12 | async-start | bytes 2228224 | tf_op jit(solution)/shard_map/reduce_scatter | solution.py:208
  422.7 242.4 %reduce-scatter.5.cloned.1.call-start = ((), (), s32[]{:S(2)}) async-start(), calls=%async_computation.10 | async-start | bytes 6684672 | tf_op jit(solution)/shard_map/reduce_scatter | solution.py:208
  436.3 284.8 %all-reduce.22.cloned.1.call-start = ((), (), s32[]{:S(2)}) async-start(), calls=%async_computation.14 | async-start | bytes 9437184 | tf_op jit(solution)/shard_map/psum | solution.py:487
  461.2 28.6 %copy-start.6 = (f32[2,512,12,64]{1,0,3,2:T(2,128)}, f32[2,512,12,64]{1,0,3,2:T(2,128)S(1)}, u32[]{:S(2)}) copy-start(f32[2,512,12,64]{1,0,3,2:T(2,128)S(1)} %reshape.615) | copy-start | bytes 9437188
  461.2 28.6 %copy-start.81 = (bf16[2,2,12]{2,1,0:T(2,128)(2,1)S(1)}, bf16[2,2,12]{2,1,0:T(2,128)(2,1)}, u32[]{:S(2)}) copy-start(bf16[2,2,12]{2,1,0:T(2,128)(2,1)} %copy-done.80) | copy-start | bytes 292
  505.6 29.9 %copy-start.83 = (pred[2,512]{1,0:T(4,128)(4,1)S(1)}, pred[2,512]{1,0:T(4,128)(4,1)}, u32[]{:S(2)}) copy-start(pred[2,512]{1,0:T(4,128)(4,1)} %copy-done.82) | copy-start | bytes 3076
  505.6 48.9 %copy-start.47 = (f32[512,32]{0,1:T(8,128)S(1)}, f32[512,32]{0,1:T(8,128)}, u32[]{:S(2)}) copy-start(f32[512,32]{0,1:T(8,128)} %copy-done.46) | copy-start | bytes 196612
  505.6 48.9 %copy-start.49 = (f32[512,32]{0,1:T(8,128)S(1)}, f32[512,32]{0,1:T(8,128)}, u32[]{:S(2)}) copy-start(f32[512,32]{0,1:T(8,128)} %copy-done.48) | copy-start | bytes 196612
  535.4 24.3 %copy-start.53 = (f32[2,512,12]{1,2,0:T(8,128)S(1)}, f32[2,512,12]{1,2,0:T(8,128)}, u32[]{:S(2)}) copy-start(f32[2,512,12]{1,2,0:T(8,128)} %copy-done.52) | copy-start | bytes 147460
  554.5 8.0 copy-start.9
  554.5 8.0 copy-start.56
  581.8 20.7 %copy-start.29 = (bf16[32,8,2,512]{3,1,2,0:T(8,128)(2,1)S(1)}, bf16[32,8,2,512]{3,1,2,0:T(8,128)(2,1)}, u32[]{:S(2)}) copy-start(bf16[32,8,2,512]{3,1,2,0:T(8,128)(2,1)} %copy.361) | copy-start | bytes 1572868
  677.9 5.6 collective-permute-start.1
  691.8 185.8 %reduce-scatter.11.cloned.1.call-start = ((), (), s32[]{:S(2)}) async-start(), calls=%async_computation.13 | async-start | bytes 5013504 | tf_op jit(solution)/shard_map/reduce_scatter | solution.py:208
  724.6 5.8 collective-permute-start.2
  (85 other events, 341.2 us)
Sparse Core Ops, SparseCore 0:
  13.1 83.2 all-gather.6
  99.7 74.5 all-gather.8
  177.6 59.2 all-gather.10
  243.0 19.8 all-reduce.17
  265.8 61.8 all-gather.12
  349.3 19.8 all-reduce.19
  415.8 15.7 reduce-scatter.6
  433.9 81.6 reduce-scatter.8
  521.7 143.3 reduce-scatter.4
  691.9 29.1 all-reduce.21
  737.8 139.7 reduce-scatter.10
